TPU v7x, 256 devices: a whole 4x4x8 slice. The times are simulated.
256 devices in a mesh: critic: 16 (over y, z_hi, core), seq: 4 (over x), tensor: 4 (over z_lo).
Axes of the slice: x: 4, y: 4, z: 8 (z_hi: 2, z_lo: 4; z = z_hi * 4 + z_lo), core: 2. Of those that a mesh axis runs over, the one named last changes fastest.
Arguments:
- observations: bfloat16 [16, 256, 2048], P('seq', 'critic', 'tensor'), may hold values from -6 to 6
- actions: bfloat16 [16, 384], P('seq', 'critic'), may hold values from -6 to 6
- lengths: int32 [16], P('seq'), may hold values from 1 to 256, as said below
- boot_mask: int32 [16, 16], P('critic', 'seq'), may hold values 0 or 1
- project_weight: bfloat16 [16, 2048, 3, 2048], P('critic', None, None, 'tensor'), may hold values from -0.125 to 0.125
- output_weight: bfloat16 [16, 2048, 2048], P('critic', 'tensor'), may hold values from -0.125 to 0.125
- action_weight: bfloat16 [16, 384, 2048], P('critic'), may hold values from -0.3125 to 0.3125
- norm_gain: float32 [16, 2048], P('critic'), may hold values from 0.5 to 1.5
- value_head: float32 [16, 2048], P('critic'), may hold values from -0.6 to 0.6
Outputs:
- q_values: float32 [16, 16], P('critic', 'seq')
- obs_grad: float32 [16, 256, 2048], P('seq', 'critic', 'tensor')
- action_grad: float32 [16, 384], P('seq', ('critic', 'tensor'))
Inputs may be any that keep to these rules, and one draw needn't show every extreme that they name: `lengths`: each sequence's number of valid history steps; later positions are padding.
All inputs are finite; a program needn't handle non-finite values. No bound on the sum of `boot_mask` on one device may be relied on, other than what follows from the above.
Results may differ from a plain program's by a relative error of at most 0.0065.
Values may be sent and summed in bfloat16 or wider, within the bound.
A program may use at most 128 MiB of HBM per device.

v0:
```python
import jax
import jax.numpy as jnp
from jax import lax
from jax.sharding import PartitionSpec as P

HEAD_DIM = 128


highest = lax.Precision.HIGHEST
norm_eps = 1e-05


def attend(query_vec, key_rows, value_rows, is_valid):
    scores = jnp.einsum(
        "shd,slhd->shl", query_vec, key_rows.astype(jnp.float32), precision=highest
    ) * HEAD_DIM ** (-0.5)
    scores = jnp.where(is_valid[:, None, :], scores, -1e30)
    attention = jax.nn.softmax(scores, axis=-1)
    attention_round = attention.astype(jnp.bfloat16)
    attended = jnp.einsum(
        "shl,slhd->shd",
        attention_round.astype(jnp.float32),
        value_rows.astype(jnp.float32),
        precision=highest,
    )
    return (
        attention,
        attention_round,
        attended.astype(jnp.bfloat16).reshape(query_vec.shape[0], -1),
    )


def attend_back(grad_heads, query_vec, key_rows, value_rows, attention, attention_round):
    value_float = value_rows.astype(jnp.float32)
    key_float = key_rows.astype(jnp.float32)
    grad_attention = jnp.einsum("shd,slhd->shl", grad_heads, value_float, precision=highest)
    grad_value = jnp.einsum(
        "shl,shd->slhd", attention_round.astype(jnp.float32), grad_heads, precision=highest
    )
    grad_scores = attention * (
        grad_attention - jnp.sum(attention * grad_attention, axis=-1, keepdims=True)
    )
    grad_query = jnp.einsum(
        "shl,slhd->shd", grad_scores, key_float, precision=highest
    ) * HEAD_DIM ** (-0.5)
    grad_key = jnp.einsum(
        "shl,shd->slhd", grad_scores, query_vec, precision=highest
    ) * HEAD_DIM ** (-0.5)
    return (grad_query, grad_key, grad_value)


def head_forward(hidden_last, gain_row, head_row):
    inverse = lax.rsqrt(jnp.mean(hidden_last * hidden_last, axis=-1, keepdims=True) + norm_eps)
    normed = hidden_last * inverse
    return (jnp.sum(head_row * gain_row * normed, axis=-1), normed, inverse)


def head_backward(weight_row, normed, inverse, gain_row, head_row):
    grad_normed = weight_row[:, None] * head_row * gain_row
    return inverse * (grad_normed - normed * jnp.mean(grad_normed * normed, axis=-1, keepdims=True))


def on_device(
    observations,
    actions,
    lengths,
    boot_mask,
    project_weight,
    output_weight,
    action_weight,
    norm_gain,
    value_head,
):
    feature_rows = lax.all_gather(observations, "tensor", axis=2, tiled=True)
    actions_all = lax.all_gather(actions, "critic", axis=1, tiled=True)
    project = project_weight[0]
    out_weight = output_weight[0]
    act_weight = action_weight[0]
    model_width = project.shape[0]
    inner_width = project.shape[2]
    head_count = inner_width // HEAD_DIM
    count_seq = observations.shape[0]
    length_hist = observations.shape[1] * lax.axis_size("critic")
    query_weight = project[:, 0]
    keyval_weight = project[:, 1:].reshape(model_width, 2 * inner_width)
    last_pos = lengths - 1
    row_ids = jnp.arange(count_seq, dtype=jnp.int32)
    positions = jnp.arange(length_hist, dtype=jnp.int32)
    is_last = positions[None, :] == last_pos[:, None]
    is_valid = positions[None, :] < lengths[:, None]
    embedded = jnp.dot(actions_all, act_weight, preferred_element_type=jnp.float32)
    full_rows = lax.all_gather(feature_rows, "critic", axis=1, tiled=True)
    last_row = full_rows[row_ids, last_pos].astype(jnp.float32) + embedded
    last_round = last_row.astype(jnp.bfloat16)
    mixed = jnp.where(is_last[:, :, None], last_round[:, None, :], full_rows)
    keyval_rows = jnp.dot(
        mixed.reshape(-1, model_width), keyval_weight, preferred_element_type=jnp.float32
    ).astype(jnp.bfloat16)
    keyval_rows = keyval_rows.reshape(count_seq, length_hist, 2 * inner_width)
    key_rows = keyval_rows[:, :, :inner_width].reshape(count_seq, length_hist, head_count, HEAD_DIM)
    value_rows = keyval_rows[:, :, inner_width:].reshape(
        count_seq, length_hist, head_count, HEAD_DIM
    )
    query_vec = jnp.dot(last_round, query_weight, preferred_element_type=jnp.float32).reshape(
        count_seq, head_count, HEAD_DIM
    )
    attention, attention_round, attended = attend(query_vec, key_rows, value_rows, is_valid)
    head_part = jnp.dot(attended, out_weight, preferred_element_type=jnp.float32)
    hidden_last = last_row + lax.psum(head_part, "tensor")
    q_vals, normed, inverse = head_forward(hidden_last, norm_gain[0], value_head[0])
    grad_last = head_backward(
        boot_mask[0].astype(jnp.float32), normed, inverse, norm_gain[0], value_head[0]
    )
    grad_heads = jnp.dot(
        grad_last, out_weight.T, precision=highest, preferred_element_type=jnp.float32
    )
    grad_heads = grad_heads.reshape(count_seq, head_count, HEAD_DIM)
    grad_query, grad_key, grad_value = attend_back(
        grad_heads, query_vec, key_rows, value_rows, attention, attention_round
    )
    grad_keyval = jnp.concatenate(
        [grad_key.reshape(-1, inner_width), grad_value.reshape(-1, inner_width)], axis=1
    ).astype(jnp.bfloat16)
    grad_mixed = jnp.dot(grad_keyval, keyval_weight.T, preferred_element_type=jnp.float32).reshape(
        count_seq, length_hist, model_width
    )
    leader = (lax.axis_index("tensor") == 0).astype(jnp.float32)
    grad_lastrow = grad_last * leader + jnp.dot(
        grad_query.reshape(count_seq, inner_width),
        query_weight.T,
        precision=highest,
        preferred_element_type=jnp.float32,
    )
    grad_lastrow = grad_lastrow + grad_mixed[row_ids, last_pos]
    grad_rows = jnp.where(is_last[:, :, None], grad_lastrow[:, None, :], grad_mixed)
    summed = lax.psum_scatter(grad_rows, "critic", scatter_dimension=1, tiled=True)
    summed = lax.psum_scatter(summed, "tensor", scatter_dimension=2, tiled=True)
    act_terms = jnp.dot(
        grad_lastrow, act_weight.T, precision=highest, preferred_element_type=jnp.float32
    )
    act_grad = lax.psum_scatter(act_terms, ("critic", "tensor"), scatter_dimension=1, tiled=True)
    return (q_vals[None, :], summed, act_grad)


def solution(mesh):
    in_specs = (
        P("seq", "critic", "tensor"),
        P("seq", "critic"),
        P("seq"),
        P("critic", "seq"),
        P("critic", None, None, "tensor"),
        P("critic", "tensor", None),
        P("critic", None, None),
        P("critic", None),
        P("critic", None),
    )
    out_specs = (P("critic", "seq"), P("seq", "critic", "tensor"), P("seq", ("critic", "tensor")))
    return jax.shard_map(
        on_device, mesh=mesh, in_specs=in_specs, out_specs=out_specs, check_vma=False
    )
```

profile of v0, /device:TPU:1, one launch (start us, length us, event | category | flops | bytes accessed | tf_op | source)
XLA Modules:
  0.0 450.1 jit_solution(10475566740261264313)
XLA Ops:
  7.2 15.6 %all_gather.9 = bf16[4,16,2048]{2,1,0:T(8,128)(2,1)} all-gather(bf16[4,16,512]{2,1,0:T(8,128)(2,1)} %param.9), channel_id=1, replica_groups=mesh['critic'=16,'seq'=4,'tensor'=4] {'tensor'}, dimensions={2}, use_global_device_ids=true | all-gather | bytes 327680 | tf_op jit(solution)/shard_map/all_gather | solution.py:74
  22.9 34.3 %all-gather = bf16[16,24,4]{1,2,0:T(4,128)(2,1)S(1)} all-gather(bf16[1,24,4]{1,2,0:T(4,128)(2,1)} %bitcast.112), channel_id=1, replica_groups=mesh['critic'=16,'seq'=4,'tensor'=4] {'critic'}, dimensions={0}, use_global_device_ids=true | all-gather | bytes 3264 | tf_op jit(solution)/shard_map/all_gather | solution.py:75
  57.2 0.1 reshape.128
  57.3 3.1 slice_bitcast_fusion
  60.4 4.0 copy.22
  64.3 3.3 fusion.47
  67.7 2.5 copy.52
  70.2 19.0 %copy.23 = bf16[2048,2,512]{2,1,0:T(2,128)(2,1)} copy(bf16[2048,2,512]{2,0,1:T(8,128)(2,1)S(1)} %get-tuple-element.7) | data formatting | bytes 8388608 | tf_op jit(solution)/shard_map/slice | solution.py:85
  89.2 7.9 %reshape.139 = bf16[2048,1024,1]{1,0,2:T(8,128)(2,1)} reshape(bf16[2048,2,512]{2,1,0:T(2,128)(2,1)} %copy.23) | data formatting | bytes 8388608 | tf_op jit(solution)/shard_map/reshape | solution.py:85
  97.1 0.1 iota_compare_fusion.1
  97.2 0.1 iota_compare_fusion
  97.3 6.6 %all-gather.3.cloned.1.call-done = bf16[4,256,2048]{2,1,0:T(8,128)(2,1)} async-done(((bf16[4,16,2048]{2,1,0:T(8,128)(2,1)}), bf16[4,256,2048]{2,1,0:T(8,128)(2,1)}) %all-gather.3.cloned.1.call-update) | async-done | bytes 4194320 | tf_op jit(solution)/shard_map/all_gather | solution.py:92
  103.9 1.4 gather_fusion
  105.4 1.7 fusion.48
  107.1 2.2 fusion.31
  109.3 2.7 broadcast_select_fusion.1
  112.0 0.8 copy-done.2
  112.8 4.7 %convolution_convert_fusion = bf16[1024,1024]{1,0:T(8,128)(2,1)S(1)} fusion(bf16[1024,2048]{1,0:T(8,128)(2,1)S(1)} %bitcast.101, bf16[2048,1024]{1,0:T(8,128)(2,1)S(1)} %bitcast.100), kind=kOutput, calls=%fused_computation.19 | convolution fusion | flops 4296015872 | bytes 10485760 | tf_op jit(solution)/shard_map/dot_general | solution.py:96
  117.5 2.4 slice_bitcast_fusion.2
  119.9 1.3 reshape.106
  121.2 2.0 multiply_reduce_fusion.1
  123.2 1.4 fusion.25
  124.6 0.2 copy.32
  124.9 1.5 fusion.20
  126.4 0.4 fusion.6
  126.7 12.5 %psum.7 = f32[4,2048]{1,0:T(4,128)S(1)} all-reduce(f32[4,2048]{1,0:T(4,128)S(1)} %fusion.6), channel_id=1, replica_groups=mesh['critic'=16,'seq'=4,'tensor'=4] {'tensor'}, use_global_device_ids=true, to_apply=%region_2.3 | all-reduce | flops 8192 | bytes 65536 | tf_op jit(solution)/shard_map/psum | solution.py:109
  139.2 0.1 multiply_reduce_fusion.5
  139.4 0.7 multiply_reduce_fusion.3
  140.1 1.7 fusion.29
  141.8 1.4 reshape.107
  143.2 1.2 multiply_reduce_fusion
  144.4 0.1 multiply_reduce_fusion.2
  144.4 0.1 subtract_multiply_fusion
  144.5 2.5 fusion.15
  147.0 1.2 concatenate.15
  148.3 1.2 concatenate.14
  149.5 0.3 copy-done.4
  149.7 10.3 %fusion.2 = f32[4,256,2048]{2,1,0:T(8,128)} fusion(bf16[2048,1024,1]{1,0,2:T(8,128)(2,1)} %reshape.139, bf16[4,256,512]{2,1,0:T(8,128)(2,1)S(1)} %copy-done.4, bf16[4,256,512]{2,1,0:T(8,128)(2,1)} %concatenate.14), kind=kOutput, calls=%fused_computation.8 | convolution fusion | flops 4299161600 | bytes 14680064 | tf_op jit(solution)/shard_map/dot_general | solution.py:124
  160.1 1.4 gather_fusion.1
  161.5 0.2 copy.41
  161.7 0.5 fusion.17
  162.2 3.3 fusion.1
  165.6 7.5 %broadcast_select_fusion = f32[4,256,2048]{2,1,0:T(8,128)} fusion(f32[4,256,2048]{2,1,0:T(8,128)} %fusion.2, f32[4,2048]{1,0:T(4,128)S(1)} %fusion.1, pred[4,256]{1,0:T(4,128)(4,1)S(1)} %iota_compare_fusion), kind=kLoop, calls=%fused_computation.3 | loop fusion | flops 2097152 | bytes 16811008 | tf_op jit(solution)/shard_map/jit(_where)/select_n | solution.py:135
  173.1 142.0 %reduce-scatter.4.cloned.1.call-done = f32[4,16,2048]{2,1,0:T(8,128)} async-done(((f32[4,256,2048]{2,1,0:T(8,128)}), f32[4,16,2048]{2,1,0:T(8,128)}) %reduce-scatter.4.cloned.1.call-update) | async-done | bytes 524304 | tf_op jit(solution)/shard_map/reduce_scatter | solution.py:136
  315.2 0.6 dynamic-slice
  316.4 2.7 fusion.10
  319.1 123.8 %all-reduce = f32[4,384]{1,0:T(4,128)S(1)} all-reduce(f32[4,384]{1,0:T(4,128)S(1)} %fusion.10), channel_id=4, replica_groups=mesh['critic'=16,'seq'=4,'tensor'=4] {'critic','tensor'}, use_global_device_ids=true, to_apply=%region_9.10.clone | all-reduce | flops 1536 | bytes 12288
  443.0 0.7 constant_dynamic-slice_fusion
  (37 shorter events, 0.3 us)
Async XLA Ops:
  7.2 119.2 %copy-start = (bf16[1,512,2048]{2,1,0:T(8,128)(2,1)S(1)}, bf16[1,512,2048]{2,1,0:T(8,128)(2,1)}, u32[]{:S(2)}) copy-start(bf16[1,512,2048]{2,1,0:T(8,128)(2,1)} %param.14) | copy-start | bytes 6291460
  7.2 96.7 %all-gather.3.cloned.1.call-start = ((), (), s32[]{:S(2)}) async-start(), calls=%async_computation.2 | async-start | bytes 4456448 | tf_op jit(solution)/shard_map/all_gather | solution.py:92
  22.9 292.2 %reduce-scatter.4.cloned.1.call-start = ((), (), s32[]{:S(2)}) async-start(), calls=%async_computation.3 | async-start | bytes 8912896 | tf_op jit(solution)/shard_map/reduce_scatter | solution.py:136
  89.2 7.9 %copy-start.5 = (f32[1,2048]{1,0:T(1,128)S(1)}, f32[1,2048]{1,0:T(1,128)}, u32[]{:S(2)}) copy-start(f32[1,2048]{1,0:T(1,128)} %param.16) | copy-start | bytes 24580
  89.2 7.9 %copy-start.6 = (f32[1,2048]{1,0:T(1,128)S(1)}, f32[1,2048]{1,0:T(1,128)}, u32[]{:S(2)}) copy-start(f32[1,2048]{1,0:T(1,128)} %param.17) | copy-start | bytes 24580
  89.2 7.9 %copy-start.8 = (s32[4]{0:T(128)S(1)}, s32[4]{0:T(128)}, u32[]{:S(2)}) copy-start(s32[4]{0:T(128)} %param.11) | copy-start | bytes 52
  89.2 7.9 %copy-start.7 = (s32[1,4]{1,0:T(1,128)S(1)}, s32[1,4]{1,0:T(1,128)}, u32[]{:S(2)}) copy-start(s32[1,4]{1,0:T(1,128)} %param.12) | copy-start | bytes 52
  109.3 3.5 copy-start.2
  148.3 1.5 copy-start.4
  149.7 12.0 %copy-start.3 = (bf16[4,32,4,8,128]{4,3,2,1,0:T(8,128)(2,1)S(1)}, bf16[4,32,4,8,128]{4,3,2,1,0:T(8,128)(2,1)}, u32[]{:S(2)}) copy-start(bf16[4,32,4,8,128]{4,3,2,1,0:T(8,128)(2,1)} %get-tuple-element.9) | copy-start | bytes 3145732
  173.0 142.1 %copy-start.9 = (u32[256]{0:T(256)S(1)}, u32[256]{0:T(256)}, u32[]{:S(2)}) copy-start(u32[256]{0:T(256)} %constant.69) | copy-start | bytes 3076
  173.0 270.6 %copy-start.1 = (bf16[1,512,2048]{2,1,0:T(8,128)(2,1)S(1)}, bf16[1,512,2048]{2,1,0:T(8,128)(2,1)}, u32[]{:S(2)}) copy-start(bf16[1,512,2048]{2,1,0:T(8,128)(2,1)} %param.14) | copy-start | bytes 6291460
  173.1 270.6 %reduce-scatter.6.cloned.1.call-start = ((), (), s32[]{:S(2)}) async-start(), calls=%async_computation.4 | async-start | bytes 655360 | tf_op jit(solution)/shard_map/reduce_scatter | solution.py:137
Sparse Core Ops, SparseCore 0:
  23.0 80.8 all-gather.2
  173.2 141.9 reduce-scatter.3
  318.2 21.4 reduce-scatter.5
where the time goes:
time: 454 us; the launch traced here: 450 us
  blocking collectives  186 us (41%)
  waiting for transfers between devices  149 us (33%)
  local copies, waits for them, and re-layouts  53 us (12%)
  matrix products  29.2 us (6%)
  other arithmetic  18.4 us (4%)
  between operations  14.6 us (3%)
    reduce_scatter x1, waiting for transfers between devices, on_device(): lax.psum_scatter(grad_rows, 'critic', scatter_dimension=1, tiled=True)  142 us
    unnamed x1, blocking collectives  124 us
    all_gather x1, blocking collectives, on_device(): actions_all = lax.all_gather(actions, 'critic', axis=1, tiled=True)  34.3 us
    slice x2, local copies, waits for them, and re-layouts, on_device(): keyval_weight = project[:, 1:].reshape(model_width, 2 * inner_width)  22.3 us
    all_gather x1, blocking collectives, on_device(): feature_rows = lax.all_gather(observations, 'tensor', axis=2, tiled=True)  15.6 us
    psum x1, blocking collectives, on_device(): hidden_last = last_row + lax.psum(head_part, 'tensor')  12.5 us
    reshape x2, local copies, waits for them, and re-layouts, on_device(): keyval_weight = project[:, 1:].reshape(model_width, 2 * inner_width)  10.4 us
    dot_general x1, matrix products, on_device(): jnp.dot(grad_keyval, keyval_weight.T, preferred_element_type=jnp.float32)  10.3 us
  transfers between devices with their start and end apart: 3, of which 2 were waited for; matrix products, arithmetic and copies ran while one was open for 10% of the time, Pallas kernels for 0%

commit v1 on v0

v1 whole, which is shorter than its diff:
```python
import functools

import jax
import jax.numpy as jnp
from jax import lax
from jax.experimental import pallas as pl
from jax.experimental.pallas import tpu as pltpu
from jax.sharding import PartitionSpec as P

HEAD_DIM = 128
NORM_EPS = 1e-05
CORES = 2
HALVES = 2

f32 = jnp.float32
bf16 = jnp.bfloat16
NN = (((1,), (0,)), ((), ()))
NT_DIMS = (((1,), (1,)), ((), ()))


def mod(value, count):
    return lax.rem(value + count, count)


def iota(shape, axis):
    return lax.broadcasted_iota(jnp.int32, shape, axis)


def split(x):
    high = x.astype(bf16).astype(f32)
    return jnp.concatenate([high, x - high], axis=0).astype(bf16)


def dot(x, w, dims=NN):
    return lax.dot_general(x, w, dims, preferred_element_type=f32)


def dot_split(x, w, dims=NN):
    rows = x.shape[0]
    both = dot(split(x), w, dims)
    return both[:rows] + both[rows:]


def dot_exact(x, w):
    rows = x.shape[0]
    high = x.astype(bf16).astype(f32)
    rest = x - high
    mid = rest.astype(bf16).astype(f32)
    terms = jnp.concatenate([high, mid, rest - mid], axis=0).astype(bf16)
    out = dot(terms, w)
    return out[:rows] + out[rows : 2 * rows] + out[2 * rows :]


def kernel(
    cfg,
    obs_hbm,
    act_ref,
    len_ref,
    boot_ref,
    project_hbm,
    out_hbm,
    actw_hbm,
    gain_ref,
    head_ref,
    q_ref,
    grad_ref,
    actgrad_ref,
    rows_all,
    weights,
    out_weight,
    act_weight,
    act_slots,
    keys,
    values,
    embedded,
    last_f32,
    last_bf,
    hid_slots,
    fact_a_src,
    fact_a,
    fact_b_src,
    fact_b,
    extra_src,
    extra,
    partial,
    sib_part,
    row_sum,
    row_parts,
    act_pick,
    act_sum,
    local_sem,
    send_sem,
    recv_sem,
):
    ny, nt, seqs, steps, feats, inner, act_len = cfg
    nz = HALVES * nt
    nyk = ny * CORES
    heads = inner // HEAD_DIM
    rows = seqs * heads
    width = nt * feats
    hist = HALVES * nyk * steps
    half = nyk * steps
    scale = HEAD_DIM ** (-0.5)

    critic = lax.axis_index("critic")
    group = lax.axis_index("tensor")
    y = lax.div(critic, HALVES * CORES)
    zh = lax.rem(lax.div(critic, CORES), HALVES)
    core = lax.rem(critic, CORES)
    z = zh * nt + group
    yk = y * CORES + core

    def dev(y_at, z_at, core_at):
        return {
            "critic": (y_at * HALVES + lax.div(z_at, nt)) * CORES + core_at,
            "tensor": lax.rem(z_at, nt),
        }

    def dev_z(z_at):
        return dev(y, z_at, core)

    def dev_yk(yk_at):
        return dev(lax.div(yk_at, CORES), z, lax.rem(yk_at, CORES))

    sibling = dev(y, z, CORES - 1 - core)

    loads = [
        pltpu.make_async_copy(src, dst, local_sem.at[i])
        for i, (src, dst) in enumerate(
            [
                (obs_hbm, rows_all.at[:, group, zh, y, core]),
                (actw_hbm, act_weight),
                (project_hbm.at[1], weights.at[1]),
                (project_hbm.at[2], weights.at[2]),
                (project_hbm.at[0], weights.at[0]),
                (out_hbm, out_weight),
            ]
        )
    ]
    for load in loads:
        load.start()

    barrier = pltpu.get_barrier_semaphore()
    for d in range(1, nz):
        pl.semaphore_signal(
            barrier, inc=1, device_id=dev_z(mod(z + d, nz)), device_id_type=pl.DeviceIdType.MESH
        )
    for d in range(1, nyk):
        pl.semaphore_signal(
            barrier, inc=1, device_id=dev_yk(mod(yk + d, nyk)), device_id_type=pl.DeviceIdType.MESH
        )

    act_slots[zh, yk] = act_ref[...]

    sends = []
    sem_at = [0]

    def copy_of(src, dst, target, sem):
        return pltpu.make_async_remote_copy(
            src_ref=src,
            dst_ref=dst,
            send_sem=send_sem.at[sem],
            recv_sem=recv_sem.at[sem],
            device_id=target,
            device_id_type=pl.DeviceIdType.MESH,
        )

    def push(src, dst, target):
        sem = sem_at[0]
        sem_at[0] += 1
        copy = copy_of(src, dst, target, sem)
        copy.start()
        sends.append(copy)
        return sem

    def arrive(dst, sem):
        copy_of(dst, dst, sibling, sem).wait_recv()

    def ring(at, count, block, target, forward, backward):
        sems = {}

        def send(step):
            if step < forward:
                ref = block(mod(at - step, count))
                sems[step, 1] = push(ref, ref, target(mod(at + 1, count)))
            if step < backward:
                ref = block(mod(at + step, count))
                sems[step, -1] = push(ref, ref, target(mod(at - 1, count)))

        def recv(step):
            got = []
            if step < forward:
                owner = mod(at - 1 - step, count)
                arrive(block(owner), sems[step, 1])
                got.append(owner)
            if step < backward:
                owner = mod(at + 1 + step, count)
                arrive(block(owner), sems[step, -1])
                got.append(owner)
            return got

        return send, recv, max(forward, backward)

    first = seqs // 2
    near = pl.ds(0, first)
    far = pl.ds(first, seqs - first)

    def near_z(z_at):
        return rows_all.at[near, lax.rem(z_at, nt), lax.div(z_at, nt), y, core]

    def near_y(y_at):
        return rows_all.at[near, :, :, y_at, core]

    def far_y(y_at):
        return rows_all.at[far, group, zh, y_at, core]

    def far_z(z_at):
        return rows_all.at[far, lax.rem(z_at, nt), lax.div(z_at, nt), :, core]

    def dev_y(y_at):
        return dev(y_at, z, core)

    pz_send, pz_recv, pz_steps = ring(z, nz, near_z, dev_z, nz // 2, (nz - 1) // 2)
    py_send, py_recv, py_steps = ring(y, ny, near_y, dev_y, ny // 2, (ny - 1) // 2)
    qy_send, qy_recv, qy_steps = ring(y, ny, far_y, dev_y, (ny - 1) // 2, ny // 2)
    qz_send, qz_recv, qz_steps = ring(z, nz, far_z, dev_z, (nz - 1) // 2, nz // 2)

    other = CORES - 1 - core

    def share_near(y_at):
        ref = near_y(y_at)
        sem = push(ref, ref, sibling)
        return rows_all.at[near, :, :, y_at, other], sem

    def share_far(z_at):
        ref = far_z(z_at)
        sem = push(ref, ref, sibling)
        return rows_all.at[far, lax.rem(z_at, nt), lax.div(z_at, nt), :, other], sem

    pl.semaphore_wait(barrier, nz - 1 + nyk - 1)
    loads[0].wait()
    act_sem = push(act_slots.at[zh, yk], act_slots.at[zh, yk], dev_z(mod(z + nt, nz)))
    pz_send(0)
    qy_send(0)

    arrive(act_slots.at[1 - zh, yk], act_sem)
    act_sems = []
    for d in range(1, nyk):
        ref = act_slots.at[:, yk]
        act_sems.append(push(ref, ref, dev_yk(mod(yk + d, nyk))))
    qy_recv(0)
    for step in range(1, qy_steps):
        qy_send(step)
    pz_recv(0)
    pz_send(1)
    for step in range(1, qy_steps):
        qy_recv(step)
    shared_far = []
    shared_near = []
    qz_send(0)
    shared_far.append(share_far(z))

    for d in range(1, nyk):
        arrive(act_slots.at[:, mod(yk - d, nyk)], act_sems[d - 1])
    act_part = act_ref.shape[1]
    gathered = jnp.zeros((16, act_weight.shape[0]), f32)
    lane = iota((act_part, act_weight.shape[0]), 1)
    lane_row = iota((act_part, act_weight.shape[0]), 0)
    for zh_at in range(HALVES):
        for yk_at in range(nyk):
            c = (yk_at // CORES * HALVES + zh_at) * CORES + yk_at % CORES
            place = (lane == lane_row + c * act_len) & (lane_row < act_len)
            gathered += dot(act_slots[zh_at, yk_at], place.astype(f32).astype(bf16))

    for step in range(1, pz_steps):
        pz_recv(step)
        if step + 1 < pz_steps:
            pz_send(step + 1)
    py_send(0)
    shared_near.append(share_near(y))
    loads[1].wait()
    embedded[...] = dot(gathered.astype(bf16), act_weight[...])

    part = act_len // nt
    pick_shape = act_pick.shape
    col = iota(pick_shape, 1)
    row = iota(pick_shape, 0)
    to_z = lax.div(col, 128)
    within = lax.rem(col, 128)
    to_yk = lax.div(within, part)
    to_critic = (lax.div(to_yk, CORES) * HALVES + lax.div(to_z, nt)) * CORES + lax.rem(to_yk, CORES)
    source = (to_critic * nt + lax.rem(to_z, nt)) * part + lax.rem(within, part)
    act_pick[...] = ((row == source) & (within < nyk * part)).astype(f32).astype(bf16)

    todo = [("q", s) for s in range(qz_steps)]
    for s in range(py_steps):
        todo.insert(2 * s + 1, ("p", s))
    for kind, step in todo:
        if kind == "q":
            got = qz_recv(step)
            if step + 1 < qz_steps:
                qz_send(step + 1)
            shared_far.extend(share_far(owner) for owner in got)
        else:
            got = py_recv(step)
            if step + 1 < py_steps:
                py_send(step + 1)
            shared_near.extend(share_near(owner) for owner in got)

    def position(index):
        zh_at = lax.div(index, half)
        yk_at = lax.div(lax.rem(index, half), steps)
        c = (lax.div(yk_at, CORES) * HALVES + zh_at) * CORES + lax.rem(yk_at, CORES)
        return c * steps + lax.rem(index, steps)

    loads[2].wait()
    loads[3].wait()
    lane_pos = position(iota((16, hist), 1))
    row_pos = position(iota((hist, 128), 0))

    def project(b):
        last = len_ref[b] - 1
        pick = (lane_pos == last).astype(f32).astype(bf16)
        is_last = row_pos == last
        blocks = [rows_all[b, g].reshape(hist, feats) for g in range(nt)]
        own = jnp.concatenate([dot(pick, block) for block in blocks], axis=1)
        full = own[0:8] + embedded[b : b + 1, :]
        last_f32[b : b + 1, :] = full[0:1]
        full_bf = full.astype(bf16).astype(f32)
        key_sum = jnp.zeros((hist, inner), f32)
        value_sum = jnp.zeros((hist, inner), f32)
        for g in range(nt):
            cut = slice(g * feats, (g + 1) * feats)
            mark = jnp.concatenate([is_last] * (feats // 128), axis=1)
            block = jnp.where(mark, full_bf[0:1, cut], blocks[g].astype(f32)).astype(bf16)
            key_sum += dot(block, weights[1, cut, :])
            value_sum += dot(block, weights[2, cut, :])
        keys[b] = key_sum.astype(bf16)
        values[b] = value_sum.astype(bf16)

    last_f32[...] = jnp.zeros_like(last_f32)
    for dst, sem in shared_near:
        arrive(dst, sem)
    for b in range(first):
        project(b)
    for dst, sem in shared_far:
        arrive(dst, sem)
    for b in range(first, seqs):
        project(b)

    loads[4].wait()
    last_rows = last_f32[...]
    last_bf[...] = jnp.concatenate([last_rows, jnp.zeros_like(last_rows)], axis=0).astype(bf16)
    query = dot(last_bf[...], weights[0])[0:8]
    row_id = iota((rows, inner), 0)
    row_head = lax.rem(row_id, heads) == lax.div(iota((rows, inner), 1), HEAD_DIM)

    def spread(x):
        out = jnp.zeros((rows, inner), f32)
        for b in range(seqs):
            out = jnp.where((lax.div(row_id, heads) == b) & row_head, x[b : b + 1, :], out)
        return out

    def fold(x):
        shape = x.shape
        seq_of = lax.div(iota(shape, 0), heads)
        out_row = iota((8, shape[1]), 0)
        out = jnp.zeros((8, shape[1]), f32)
        for b in range(seqs):
            total = jnp.sum(jnp.where(seq_of == b, x, 0.0), axis=0, keepdims=True)
            out = jnp.where(out_row == b, total, out)
        return out

    def per_seq(shape, make):
        seq_of = lax.div(iota(shape, 0), heads)
        out = jnp.zeros(shape, f32)
        for b in range(seqs):
            out = jnp.where(seq_of == b, make(b), out)
        return out

    query_rows = spread(query)
    scores = per_seq((rows, hist), lambda b: dot_split(query_rows, keys[b], NT_DIMS)) * scale
    seq_row = lax.div(iota((rows, hist), 0), heads)
    pos = position(iota((rows, hist), 1))
    length = jnp.zeros((rows, hist), jnp.int32)
    for b in range(seqs):
        length = jnp.where(seq_row == b, len_ref[b], length)
    scores = jnp.where(pos < length, scores, -1e30)
    weight = jnp.exp(scores - jnp.max(scores, axis=1, keepdims=True))
    weight = jnp.where(pos < length, weight, 0.0)
    attention = weight / jnp.sum(weight, axis=1, keepdims=True)
    attention_round = attention.astype(bf16)
    attended = per_seq((rows, inner), lambda b: dot(attention_round, values[b]))
    attended = fold(jnp.where(row_head, attended, 0.0))
    loads[5].wait()
    attended_bf = jnp.concatenate([attended, jnp.zeros_like(attended)], axis=0).astype(bf16)
    head_part = dot(attended_bf, out_weight[...])
    hid_slots[group, 0:seqs, :] = head_part[0:seqs, : width // 2]
    hid_slots[group, seqs : 2 * seqs, :] = head_part[0:seqs, width // 2 :]
    hid_sems = []
    for d in range(1, nt):
        to = mod(group + d, nt)
        hid_sems.append(push(hid_slots.at[group], hid_slots.at[group], dev_z(zh * nt + to)))

    key_vec = dot_split(query_rows, weights[1], NT_DIMS) * scale
    for z_at in range(nz):
        g = z_at % nt
        h = z_at // nt
        fact_a_src[z_at, :, :feats] = key_vec[:, g * feats : (g + 1) * feats].astype(bf16)
        fact_a_src[z_at, :, feats:] = attention_round[:, h * half : (h + 1) * half]
    fact_a[z] = fact_a_src[z]
    a_sems = []
    for d in range(1, nz):
        to = mod(z + d, nz)
        a_sems.append(push(fact_a_src.at[to], fact_a.at[z], dev_z(to)))

    for d in range(1, nt):
        arrive(hid_slots.at[mod(group - d, nt)], hid_sems[d - 1])
    total = hid_slots[0]
    for g in range(1, nt):
        total = total + hid_slots[g]
    zero_rows = jnp.zeros((8 - seqs, width), f32)
    head_sum = jnp.concatenate([total[0:seqs], total[seqs : 2 * seqs]], axis=1)
    hidden = last_rows + jnp.concatenate([head_sum, zero_rows], axis=0)
    gain_head = gain_ref[...] * head_ref[...]
    inverse = lax.rsqrt(jnp.sum(hidden * hidden, axis=1, keepdims=True) * (1.0 / width) + NORM_EPS)
    normed = hidden * inverse
    q_vals = jnp.sum(gain_head * normed, axis=1, keepdims=True)
    q_lane = iota((8, 128), 1)
    q_row = iota((8, 128), 0)
    q_line = jnp.sum(jnp.where(q_lane == q_row, q_vals, 0.0), axis=0, keepdims=True)
    q_ref[...] = q_line[:, 0:seqs]
    boot = jnp.zeros((8, 1), f32)
    for b in range(seqs):
        boot = jnp.where(iota((8, 1), 0) == b, boot_ref[0, b].astype(f32), boot)
    grad_normed = boot * gain_head
    mean = jnp.sum(grad_normed * normed, axis=1, keepdims=True) * (1.0 / width)
    grad_last = inverse * (grad_normed - normed * mean)

    grad_heads = spread(dot_split(grad_last, out_weight[...], NT_DIMS))
    value_vec = dot_split(grad_heads, weights[2], NT_DIMS)
    grad_attention = per_seq((rows, hist), lambda b: dot_split(grad_heads, values[b], NT_DIMS))
    grad_scores = attention * (
        grad_attention - jnp.sum(attention * grad_attention, axis=1, keepdims=True)
    )
    for z_at in range(nz):
        g = z_at % nt
        h = z_at // nt
        fact_b_src[z_at, :, :feats] = value_vec[:, g * feats : (g + 1) * feats].astype(bf16)
        fact_b_src[z_at, :, feats:] = grad_scores[:, h * half : (h + 1) * half].astype(bf16)
    fact_b[z] = fact_b_src[z]
    b_sems = []
    for d in range(1, nz):
        to = mod(z + d, nz)
        b_sems.append(push(fact_b_src.at[to], fact_b.at[z], dev_z(to)))

    grad_query = per_seq((rows, inner), lambda b: dot_split(grad_scores, keys[b]))
    grad_query = fold(jnp.where(row_head, grad_query, 0.0)) * scale
    from_query = dot_split(grad_query, weights[0], NT_DIMS)
    extra_rows = from_query + jnp.where(group == 0, 1.0, 0.0) * grad_last
    at_last = pos == length - 1
    score_last = jnp.sum(jnp.where(at_last, grad_scores, 0.0), axis=1, keepdims=True)
    weight_last = jnp.sum(
        jnp.where(at_last, attention_round.astype(f32), 0.0), axis=1, keepdims=True
    )
    grad_lastrow = extra_rows + fold(score_last * key_vec + weight_last * value_vec)
    act_terms = dot_split(grad_lastrow, act_weight[...], NT_DIMS)
    act_cols = dot_exact(act_terms, act_pick[...])
    cut = feats // 2
    for z_at in range(nz):
        g = z_at % nt
        extra_src[z_at, 0:seqs, :cut] = extra_rows[0:seqs, g * feats : g * feats + cut]
        extra_src[z_at, seqs : 2 * seqs, :cut] = extra_rows[0:seqs, g * feats + cut : (g + 1) * feats]
        extra_src[z_at, :, cut:] = act_cols[:, z_at * 128 : (z_at + 1) * 128]
    extra[z] = extra_src[z]
    x_sems = []
    for d in range(1, nz):
        to = mod(z + d, nz)
        x_sems.append(push(extra_src.at[to], extra.at[z], dev_z(to)))

    for d in range(1, nz):
        arrive(fact_a.at[mod(z - d, nz)], a_sems[d - 1])
    for d in range(1, nz):
        arrive(fact_b.at[mod(z - d, nz)], b_sems[d - 1])
    factors = nz * rows
    vec_a = fact_a[:, :, :feats].reshape(factors, feats)
    vec_b = fact_b[:, :, :feats].reshape(factors, feats)
    coef_a = fact_b[:, :, feats:].reshape(factors, half).astype(f32)
    coef_b = fact_a[:, :, feats:].reshape(factors, half).astype(f32)
    coefs = jnp.concatenate([coef_a.T, coef_b.T], axis=1)
    vecs = jnp.concatenate([vec_a, vec_b], axis=0)
    seq_col = lax.div(lax.rem(iota(coefs.shape, 1), rows), heads)
    for d in range(1, nz):
        arrive(extra.at[mod(z - d, nz)], x_sems[d - 1])
    extra_sum = extra[0]
    for z_at in range(1, nz):
        extra_sum = extra_sum + extra[z_at]
    act_sum[yk] = extra_sum[:, cut:]
    act_sems = []
    for d in range(1, nyk):
        act_sems.append(push(act_sum.at[yk], act_sum.at[yk], dev_yk(mod(yk + d, nyk))))
    extra_full = jnp.concatenate([extra_sum[0:seqs, :cut], extra_sum[seqs : 2 * seqs, :cut]], axis=1)
    here = position(iota((half, feats), 0) + zh * half)
    for b in range(seqs):
        out = dot(jnp.where(seq_col == b, coefs, 0.0).astype(bf16), vecs)
        out = out + jnp.where(here == len_ref[b] - 1, extra_full[b : b + 1, :], 0.0)
        partial[:, :, b] = out.reshape(ny, CORES, steps, feats)

    sib_sem = push(partial.at[:, other], sib_part, sibling)
    arrive(sib_part, sib_sem)
    row_sum[...] = partial[:, core] + sib_part[...]
    y_sems = []
    for d in range(1, ny):
        to = mod(y + d, ny)
        y_sems.append(push(row_sum.at[to], row_parts.at[d - 1], dev_y(to)))
    for d in range(1, nyk):
        arrive(act_sum.at[mod(yk - d, nyk)], act_sems[d - 1])
    act_total = act_sum[0]
    for yk_at in range(1, nyk):
        act_total = act_total + act_sum[yk_at]
    mine = (iota((128, 128), 0) == iota((128, 128), 1) + yk * part) & (iota((128, 128), 1) < part)
    act_mine = dot_exact(act_total, mine.astype(f32).astype(bf16))
    actgrad_ref[...] = act_mine[0:seqs, 0:part]
    result = row_sum[y]
    for d in range(1, ny):
        arrive(row_parts.at[d - 1], y_sems[d - 1])
        result = result + row_parts[d - 1]
    grad_ref[...] = result
    for copy in sends:
        copy.wait_send()


def solution(mesh):
    nt = mesh.shape["tensor"]
    ny = mesh.shape["critic"] // (HALVES * CORES)
    nz = HALVES * nt
    nyk = ny * CORES

    def on_device(obs, actions, lengths, boot, project, out_weight, act_weight, gain, head):
        seqs, steps, feats = obs.shape
        width, inner = project.shape[1], project.shape[3]
        act_len = actions.shape[1]
        rows = seqs * (inner // HEAD_DIM)
        hist = steps * HALVES * nyk
        half = steps * nyk
        weights = jnp.transpose(project[0], (1, 0, 2))
        padded = jnp.pad(actions, ((0, 16 - seqs), (0, 128 - act_len)))
        vmem = pl.BlockSpec(memory_space=pltpu.VMEM)
        smem = pl.BlockSpec(memory_space=pltpu.SMEM)
        hbm = pl.BlockSpec(memory_space=pl.ANY)
        part = act_len // nt
        flops = 4 * seqs * hist * width * inner
        return pl.pallas_call(
            functools.partial(kernel, (ny, nt, seqs, steps, feats, inner, act_len)),
            out_shape=(
                jax.ShapeDtypeStruct((1, seqs), f32),
                jax.ShapeDtypeStruct((seqs, steps, feats), f32),
                jax.ShapeDtypeStruct((seqs, part), f32),
            ),
            in_specs=[hbm, vmem, smem, smem, hbm, hbm, hbm, vmem, vmem],
            out_specs=(vmem, vmem, vmem),
            scratch_shapes=[
                pltpu.VMEM((seqs, nt, HALVES, ny, CORES, steps, feats), bf16),
                pltpu.VMEM((3, width, inner), bf16),
                pltpu.VMEM((inner, width), bf16),
                pltpu.VMEM(act_weight.shape[1:], bf16),
                pltpu.VMEM((HALVES, nyk, 16, 128), bf16),
                pltpu.VMEM((seqs, hist, inner), bf16),
                pltpu.VMEM((seqs, hist, inner), bf16),
                pltpu.VMEM((16, width), f32),
                pltpu.VMEM((8, width), f32),
                pltpu.VMEM((16, width), bf16),
                pltpu.VMEM((nt, 8, width // 2), f32),
                pltpu.VMEM((nz, rows, feats + half), bf16),
                pltpu.VMEM((nz, rows, feats + half), bf16),
                pltpu.VMEM((nz, rows, feats + half), bf16),
                pltpu.VMEM((nz, rows, feats + half), bf16),
                pltpu.VMEM((nz, 8, feats // 2 + 128), f32),
                pltpu.VMEM((nz, 8, feats // 2 + 128), f32),
                pltpu.VMEM((ny, CORES, seqs, steps, feats), f32),
                pltpu.VMEM((ny, seqs, steps, feats), f32),
                pltpu.VMEM((ny, seqs, steps, feats), f32),
                pltpu.VMEM((ny - 1, seqs, steps, feats), f32),
                pltpu.VMEM((act_weight.shape[1], nz * 128), bf16),
                pltpu.VMEM((nyk, 8, 128), f32),
                pltpu.SemaphoreType.DMA((6,)),
                pltpu.SemaphoreType.DMA((96,)),
                pltpu.SemaphoreType.DMA((96,)),
            ],
            compiler_params=pltpu.CompilerParams(
                collective_id=0, has_side_effects=True, vmem_limit_bytes=48 * 1024 * 1024
            ),
            cost_estimate=pl.CostEstimate(
                flops=flops, bytes_accessed=10 * 1024 * 1024, transcendentals=seqs * hist
            ),
        )(obs, padded, lengths, boot, weights, out_weight[0], act_weight[0], gain, head)

    in_specs = (
        P("seq", "critic", "tensor"),
        P("seq", "critic"),
        P("seq"),
        P("critic", "seq"),
        P("critic", None, None, "tensor"),
        P("critic", "tensor", None),
        P("critic", None, None),
        P("critic", None),
        P("critic", None),
    )
    out_specs = (P("critic", "seq"), P("seq", "critic", "tensor"), P("seq", ("critic", "tensor")))
    return jax.shard_map(
        on_device, mesh=mesh, in_specs=in_specs, out_specs=out_specs, check_vma=False
    )
```

time: 454 us -> 86.6 us (0.19)
  blocking collectives: 186 us -> 0 us
  waiting for transfers between devices: 149 us -> 0 us
  Pallas kernels: 0 us -> 76.7 us
  local copies, waits for them, and re-layouts: 53 us -> 8.97 us
  matrix products: 29.2 us -> 0 us
  other arithmetic: 18.4 us -> 0 us
  between operations: 14.6 us -> 0.65 us
    reduce_scatter x2 -> x0, waiting for transfers between devices: 142 us -> none  [the longest x1 142 us: on_device(): lax.psum_scatter(grad_rows, 'critic', scatter_dimension=1, tiled=True)]
    unnamed x1 -> x0, blocking collectives: 124 us -> none
    pallas_call x0 -> x1, Pallas kernels: none -> 76.7 us  [on_device(): pl.pallas_call(functools.partial(kernel, (ny, nt, seqs, steps, feats, inn...]
    all_gather x2 -> x0, blocking collectives: 49.9 us -> none  [the longest x1 34.3 us: on_device(): actions_all = lax.all_gather(actions, 'critic', axis=1, tiled=True)]
    dot_general x10 -> x0, matrix products: 29.2 us -> none  [the longest x1 10.3 us: on_device(): jnp.dot(grad_keyval, keyval_weight.T, preferred_element_type=jnp.float32)]
    slice x2 -> x0, local copies, waits for them, and re-layouts: 22.3 us -> none  [on_device(): keyval_weight = project[:, 1:].reshape(model_width, 2 * inner_width)]
    reshape x4 -> x0, local copies, waits for them, and re-layouts: 13 us -> none  [the longest x2 10.4 us: on_device(): keyval_weight = project[:, 1:].reshape(model_width, 2 * inner_width)]
    psum x1 -> x0, blocking collectives: 12.5 us -> none  [on_device(): hidden_last = last_row + lax.psum(head_part, 'tensor')]
  transfers between devices with their start and end apart: 3 -> 0, of which waited for: 2 -> 0; matrix products, arithmetic and copies ran while one was open for 10% -> 0% of each run, Pallas kernels for 0% -> 0%
where the time goes in v1:
time: 86.6 us; the launch traced here: 86.3 us
  Pallas kernels  76.7 us (89%)
  local copies, waits for them, and re-layouts  8.97 us (10%)
    pallas_call x1, Pallas kernels, on_device(): pl.pallas_call(functools.partial(kernel, (ny, nt, seqs, steps, feats, inn...  76.7 us
    unnamed x17, local copies, waits for them, and re-layouts  8.28 us

profile of v1, /device:TPU:1, one launch (start us, length us, event | category | flops | bytes accessed | tf_op | source)
XLA Modules:
  0.0 86.3 jit_solution(10006592057695633002)
XLA Ops:
  0.6 0.7 pad.4.act_ref
  1.3 0.0 copy-start
  1.3 1.6 %copy-done = bf16[1,512,2048]{2,1,0:T(8,128)(2,1)S(1)} copy-done((bf16[1,512,2048]{2,1,0:T(8,128)(2,1)S(1)}, bf16[1,512,2048]{2,1,0:T(8,128)(2,1)}, u32[]{:S(2)}) %copy-start) | copy-done | bytes 2097176
  2.9 0.0 copy-start.1
  2.9 1.4 %copy-done.1 = bf16[1,384,2048]{2,1,0:T(8,128)(2,1)S(1)} copy-done((bf16[1,384,2048]{2,1,0:T(8,128)(2,1)S(1)}, bf16[1,384,2048]{2,1,0:T(8,128)(2,1)}, u32[]{:S(2)}) %copy-start.1) | copy-done | bytes 1572888
  4.3 0.0 copy-start.2
  4.3 0.8 copy-done.2
  5.2 0.0 copy-start.3
  5.2 0.7 copy-done.3
  5.9 0.0 copy-start.4
  5.9 0.7 copy-done.4
  6.6 0.0 copy-start.5
  6.6 0.7 copy-done.5
  7.2 0.0 copy-start.6
  7.2 0.7 copy-done.6
  7.9 76.7 %shard_map.112 = (f32[1,4]{1,0:T(1,128)S(1)}, f32[4,16,512]{2,1,0:T(8,128)S(1)}, f32[4,6]{1,0:T(4,128)S(1)}) custom-call(bf16[4,16,512]{2,1,0:T(8,128)(2,1)S(1)} %copy-done.2, bf16[16,128]{1,0:T(8,128)(2,1)S(1)} %pad.4.act_ref, s32[4]{0:T(128)S(1)} %copy-done.5, s32[1,4]{1,0:T(1,128)S(1)} %copy-done.6, bf16[3,2048,512]{2,1,0:T(8,128)(2,1)} %bitcast.7, ...), custom_call_target="tpu_custom_call" | custom-call | flops 4294967296 | bytes 10485760 | tf_op jit(solution)/shard_map/pallas_call | solution.py:553
  84.6 0.5 copy.15
  85.1 0.7 copy.16
  85.7 0.6 copy.17
Async XLA Ops:
  1.3 1.6 %copy-start = (bf16[1,512,2048]{2,1,0:T(8,128)(2,1)S(1)}, bf16[1,512,2048]{2,1,0:T(8,128)(2,1)}, u32[]{:S(2)}) copy-start(bf16[1,512,2048]{2,1,0:T(8,128)(2,1)} %param.14) | copy-start | bytes 6291460
  2.9 1.4 %copy-start.1 = (bf16[1,384,2048]{2,1,0:T(8,128)(2,1)S(1)}, bf16[1,384,2048]{2,1,0:T(8,128)(2,1)}, u32[]{:S(2)}) copy-start(bf16[1,384,2048]{2,1,0:T(8,128)(2,1)} %param.15) | copy-start | bytes 4718596
  4.3 0.8 copy-start.2
  5.2 0.7 copy-start.3
  5.9 0.7 copy-start.4
  6.6 0.7 copy-start.5
  7.2 0.7 copy-start.6

commit v2 on v1

--- a/solution.py
+++ b/solution.py
@@ -54,14 +54,14 @@
 def kernel(
     cfg,
     obs_hbm,
-    act_ref,
-    len_ref,
-    boot_ref,
+    act_hbm,
+    len_hbm,
+    boot_hbm,
     project_hbm,
     out_hbm,
     actw_hbm,
-    gain_ref,
-    head_ref,
+    gain_hbm,
+    head_hbm,
     q_ref,
     grad_ref,
     actgrad_ref,
@@ -88,6 +88,10 @@
     row_parts,
     act_pick,
     act_sum,
+    len_ref,
+    boot_ref,
+    gain_ref,
+    head_ref,
     local_sem,
     send_sem,
     recv_sem,
@@ -134,6 +138,11 @@
                 (project_hbm.at[2], weights.at[2]),
                 (project_hbm.at[0], weights.at[0]),
                 (out_hbm, out_weight),
+                (act_hbm, act_slots.at[zh, yk]),
+                (len_hbm, len_ref),
+                (boot_hbm, boot_ref),
+                (gain_hbm, gain_ref),
+                (head_hbm, head_ref),
             ]
         )
     ]
@@ -150,7 +159,16 @@
             barrier, inc=1, device_id=dev_yk(mod(yk + d, nyk)), device_id_type=pl.DeviceIdType.MESH
         )
 
-    act_slots[zh, yk] = act_ref[...]
+    part = act_len // nt
+    pick_shape = act_pick.shape
+    col = iota(pick_shape, 1)
+    row = iota(pick_shape, 0)
+    to_z = lax.div(col, 128)
+    within = lax.rem(col, 128)
+    to_yk = lax.div(within, part)
+    to_critic = (lax.div(to_yk, CORES) * HALVES + lax.div(to_z, nt)) * CORES + lax.rem(to_yk, CORES)
+    source = (to_critic * nt + lax.rem(to_z, nt)) * part + lax.rem(within, part)
+    act_pick[...] = ((row == source) & (within < nyk * part)).astype(f32).astype(bf16)
 
     sends = []
     sem_at = [0]
@@ -204,108 +222,104 @@
     first = seqs // 2
     near = pl.ds(0, first)
     far = pl.ds(first, seqs - first)
-
-    def near_z(z_at):
-        return rows_all.at[near, lax.rem(z_at, nt), lax.div(z_at, nt), y, core]
-
-    def near_y(y_at):
-        return rows_all.at[near, :, :, y_at, core]
-
-    def far_y(y_at):
-        return rows_all.at[far, group, zh, y_at, core]
-
-    def far_z(z_at):
-        return rows_all.at[far, lax.rem(z_at, nt), lax.div(z_at, nt), :, core]
+    other = CORES - 1 - core
+
+    def block_at(part, z_at, y_at):
+        return rows_all.at[part, lax.rem(z_at, nt), lax.div(z_at, nt), y_at, core]
 
     def dev_y(y_at):
         return dev(y_at, z, core)
 
-    pz_send, pz_recv, pz_steps = ring(z, nz, near_z, dev_z, nz // 2, (nz - 1) // 2)
-    py_send, py_recv, py_steps = ring(y, ny, near_y, dev_y, ny // 2, (ny - 1) // 2)
-    qy_send, qy_recv, qy_steps = ring(y, ny, far_y, dev_y, (ny - 1) // 2, ny // 2)
-    qz_send, qz_recv, qz_steps = ring(z, nz, far_z, dev_z, (nz - 1) // 2, nz // 2)
-
-    other = CORES - 1 - core
-
-    def share_near(y_at):
-        ref = near_y(y_at)
+    def share(part, z_at):
+        ref = rows_all.at[part, lax.rem(z_at, nt), lax.div(z_at, nt), :, core]
         sem = push(ref, ref, sibling)
-        return rows_all.at[near, :, :, y_at, other], sem
-
-    def share_far(z_at):
-        ref = far_z(z_at)
-        sem = push(ref, ref, sibling)
-        return rows_all.at[far, lax.rem(z_at, nt), lax.div(z_at, nt), :, other], sem
+        return rows_all.at[part, lax.rem(z_at, nt), lax.div(z_at, nt), :, other], sem
+
+    shared_near = []
+    shared_far = []
+    act_sems = []
+    steps_up = nz // 2
+    steps_down = (nz - 1) // 2
+    near_ring = ring(z, nz, lambda z_at: block_at(near, z_at, y), dev_z, steps_up, steps_down)
+    far_rings = []
+    for d in range(ny):
+        y_at = mod(y - d, ny)
+        ups, downs = (steps_up, steps_down) if d % 2 else (steps_down, steps_up)
+        far_rings.append(
+            ring(z, nz, functools.partial(lambda y_at, z_at: block_at(far, z_at, y_at), y_at), dev_z, ups, downs)
+        )
+    ring_steps = max(steps_up, steps_down)
+
+    def spread_y(z_at):
+        ref = block_at(near, z_at, y)
+        return z_at, [push(ref, ref, dev_y(mod(y + d, ny))) for d in range(1, ny)]
+
+    def finish_near(owner, sems):
+        for d, sem in zip(range(1, ny), sems):
+            arrive(block_at(near, owner, mod(y - d, ny)), sem)
+        shared_near.append(share(near, owner))
+
+    def prepare_actions():
+        for d in range(1, nyk):
+            arrive(act_slots.at[:, mod(yk - d, nyk)], act_sems[d - 1])
+        act_part = act_slots.shape[3]
+        gathered = jnp.zeros((16, act_weight.shape[0]), f32)
+        lane = iota((act_part, act_weight.shape[0]), 1)
+        lane_row = iota((act_part, act_weight.shape[0]), 0)
+        for zh_at in range(HALVES):
+            for yk_at in range(nyk):
+                c = (yk_at // CORES * HALVES + zh_at) * CORES + yk_at % CORES
+                place = (lane == lane_row + c * act_len) & (lane_row < act_len)
+                gathered += dot(act_slots[zh_at, yk_at], place.astype(f32).astype(bf16))
+
+        loads[1].wait()
+        embedded[...] = dot(gathered.astype(bf16), act_weight[...])
 
     pl.semaphore_wait(barrier, nz - 1 + nyk - 1)
     loads[0].wait()
+    near_send, near_recv, _ = near_ring
+    near_send(0)
+    far_rings[0][0](0)
+    far_y = []
+    for d in range(1, ny):
+        ref = block_at(far, z, y)
+        far_y.append(push(ref, ref, dev_y(mod(y + d, ny))))
+    waiting = [spread_y(z)]
+    loads[6].wait()
     act_sem = push(act_slots.at[zh, yk], act_slots.at[zh, yk], dev_z(mod(z + nt, nz)))
-    pz_send(0)
-    qy_send(0)
-
-    arrive(act_slots.at[1 - zh, yk], act_sem)
-    act_sems = []
-    for d in range(1, nyk):
-        ref = act_slots.at[:, yk]
-        act_sems.append(push(ref, ref, dev_yk(mod(yk + d, nyk))))
-    qy_recv(0)
-    for step in range(1, qy_steps):
-        qy_send(step)
-    pz_recv(0)
-    pz_send(1)
-    for step in range(1, qy_steps):
-        qy_recv(step)
-    shared_far = []
-    shared_near = []
-    qz_send(0)
-    shared_far.append(share_far(z))
-
-    for d in range(1, nyk):
-        arrive(act_slots.at[:, mod(yk - d, nyk)], act_sems[d - 1])
-    act_part = act_ref.shape[1]
-    gathered = jnp.zeros((16, act_weight.shape[0]), f32)
-    lane = iota((act_part, act_weight.shape[0]), 1)
-    lane_row = iota((act_part, act_weight.shape[0]), 0)
-    for zh_at in range(HALVES):
-        for yk_at in range(nyk):
-            c = (yk_at // CORES * HALVES + zh_at) * CORES + yk_at % CORES
-            place = (lane == lane_row + c * act_len) & (lane_row < act_len)
-            gathered += dot(act_slots[zh_at, yk_at], place.astype(f32).astype(bf16))
-
-    for step in range(1, pz_steps):
-        pz_recv(step)
-        if step + 1 < pz_steps:
-            pz_send(step + 1)
-    py_send(0)
-    shared_near.append(share_near(y))
-    loads[1].wait()
-    embedded[...] = dot(gathered.astype(bf16), act_weight[...])
-
-    part = act_len // nt
-    pick_shape = act_pick.shape
-    col = iota(pick_shape, 1)
-    row = iota(pick_shape, 0)
-    to_z = lax.div(col, 128)
-    within = lax.rem(col, 128)
-    to_yk = lax.div(within, part)
-    to_critic = (lax.div(to_yk, CORES) * HALVES + lax.div(to_z, nt)) * CORES + lax.rem(to_yk, CORES)
-    source = (to_critic * nt + lax.rem(to_z, nt)) * part + lax.rem(within, part)
-    act_pick[...] = ((row == source) & (within < nyk * part)).astype(f32).astype(bf16)
-
-    todo = [("q", s) for s in range(qz_steps)]
-    for s in range(py_steps):
-        todo.insert(2 * s + 1, ("p", s))
-    for kind, step in todo:
-        if kind == "q":
-            got = qz_recv(step)
-            if step + 1 < qz_steps:
-                qz_send(step + 1)
-            shared_far.extend(share_far(owner) for owner in got)
-        else:
-            got = py_recv(step)
-            if step + 1 < py_steps:
-                py_send(step + 1)
-            shared_near.extend(share_near(owner) for owner in got)
+    for d in range(1, ny):
+        arrive(block_at(far, z, mod(y - d, ny)), far_y[d - 1])
+        far_rings[d][0](0)
+    shared_far.append(share(far, z))
+    for step in range(ring_steps):
+        got = near_recv(step)
+        if step + 1 < ring_steps:
+            near_send(step + 1)
+        came = [spread_y(owner) for owner in got]
+        far_got = []
+        for send, recv, _ in far_rings:
+            owners = recv(step)
+            if step + 1 < ring_steps:
+                send(step + 1)
+            far_got = owners if len(owners) > len(far_got) else far_got
+        if step + 1 < ring_steps:
+            shared_far.extend(share(far, owner) for owner in far_got)
+        for item in waiting:
+            finish_near(*item)
+        waiting = came
+        if step == 0:
+            arrive(act_slots.at[1 - zh, yk], act_sem)
+            for d in range(1, nyk):
+                ref = act_slots.at[:, yk]
+                act_sems.append(push(ref, ref, dev_yk(mod(yk + d, nyk))))
+        if step == 2:
+            prepare_actions()
+    for item in waiting:
+        finish_near(*item)
+    if steps_up == steps_down:
+        shared_far.extend(share(far, owner) for owner in far_got)
+    else:
+        shared_far.append(share(far, mod(z + ring_steps, nz)))
 
     def position(index):
         zh_at = lax.div(index, half)
@@ -313,8 +327,8 @@
         c = (lax.div(yk_at, CORES) * HALVES + zh_at) * CORES + lax.rem(yk_at, CORES)
         return c * steps + lax.rem(index, steps)
 
-    loads[2].wait()
-    loads[3].wait()
+    for load in loads[2:4] + loads[7:]:
+        load.wait()
     lane_pos = position(iota((16, hist), 1))
     row_pos = position(iota((hist, 128), 0))
 
@@ -546,8 +560,7 @@
         weights = jnp.transpose(project[0], (1, 0, 2))
         padded = jnp.pad(actions, ((0, 16 - seqs), (0, 128 - act_len)))
         vmem = pl.BlockSpec(memory_space=pltpu.VMEM)
-        smem = pl.BlockSpec(memory_space=pltpu.SMEM)
-        hbm = pl.BlockSpec(memory_space=pl.ANY)
+        hbm = pl.BlockSpec(memory_space=pltpu.HBM)
         part = act_len // nt
         flops = 4 * seqs * hist * width * inner
         return pl.pallas_call(
@@ -557,7 +570,7 @@
                 jax.ShapeDtypeStruct((seqs, steps, feats), f32),
                 jax.ShapeDtypeStruct((seqs, part), f32),
             ),
-            in_specs=[hbm, vmem, smem, smem, hbm, hbm, hbm, vmem, vmem],
+            in_specs=[hbm] * 9,
             out_specs=(vmem, vmem, vmem),
             scratch_shapes=[
                 pltpu.VMEM((seqs, nt, HALVES, ny, CORES, steps, feats), bf16),
@@ -583,12 +596,16 @@
                 pltpu.VMEM((ny - 1, seqs, steps, feats), f32),
                 pltpu.VMEM((act_weight.shape[1], nz * 128), bf16),
                 pltpu.VMEM((nyk, 8, 128), f32),
-                pltpu.SemaphoreType.DMA((6,)),
-                pltpu.SemaphoreType.DMA((96,)),
-                pltpu.SemaphoreType.DMA((96,)),
+                pltpu.SMEM((seqs,), jnp.int32),
+                pltpu.SMEM((1, seqs), jnp.int32),
+                pltpu.VMEM((1, width), f32),
+                pltpu.VMEM((1, width), f32),
+                pltpu.SemaphoreType.DMA((11,)),
+                pltpu.SemaphoreType.DMA((160,)),
+                pltpu.SemaphoreType.DMA((160,)),
             ],
             compiler_params=pltpu.CompilerParams(
-                collective_id=0, has_side_effects=True, vmem_limit_bytes=48 * 1024 * 1024
+                collective_id=0, has_side_effects=True, vmem_limit_bytes=63 * 1024 * 1024
             ),
             cost_estimate=pl.CostEstimate(
                 flops=flops, bytes_accessed=10 * 1024 * 1024, transcendentals=seqs * hist

time: 86.6 us -> 72.9 us (0.84)
  Pallas kernels: 76.7 us -> 66.6 us
  local copies, waits for them, and re-layouts: 8.97 us -> 5.27 us
    pallas_call x1, Pallas kernels: 76.7 us -> 66.6 us  [on_device(): pl.pallas_call(functools.partial(kernel, (ny, nt, seqs, steps, feats, inn...]
    unnamed x17 -> x3, local copies, waits for them, and re-layouts: 8.28 us -> 3.99 us
where the time goes in v2:
time: 72.9 us; the launch traced here: 72.6 us
  Pallas kernels  66.6 us (91%)
  local copies, waits for them, and re-layouts  5.27 us (7%)
    pallas_call x1, Pallas kernels, on_device(): pl.pallas_call(functools.partial(kernel, (ny, nt, seqs, steps, feats, inn...  66.6 us
    unnamed x3, local copies, waits for them, and re-layouts  3.99 us

profile of v2, /device:TPU:1, one launch (start us, length us, event | category | flops | bytes accessed | tf_op | source)
XLA Modules:
  0.0 72.6 jit_solution(582362245644195017)
XLA Ops:
  0.6 1.3 %pad.4.act_hbm = bf16[16,128]{1,0:T(8,128)(2,1)} pad(bf16[4,24]{1,0:T(4,128)(2,1)} %param.10, bf16[]{:T(256)} %constant.2.clone.1), padding=0_12x0_104 | pad | bytes 4290 | tf_op jit(solution)/shard_map/jit(_pad)/pad | solution.py:561
  1.9 66.6 %shard_map.112 = (f32[1,4]{1,0:T(1,128)}, f32[4,16,512]{2,1,0:T(8,128)}, f32[4,6]{1,0:T(4,128)}) custom-call(bf16[4,16,512]{2,1,0:T(8,128)(2,1)} %obs_hbm.1, bf16[16,128]{1,0:T(8,128)(2,1)} %pad.4.act_hbm, s32[4]{0:T(128)} %len_hbm.1, s32[1,4]{1,0:T(1,128)} %boot_hbm.1, bf16[3,2048,512]{2,1,0:T(8,128)(2,1)} %bitcast.5, bf16[512,2048]{1,0:T(8,128)(2,1)} %bitcast.6, ...), custom_call_target="tpu_custom_call" | custom-call | flops 4294967296 | bytes 10485760 | tf_op jit(solution)/shard_map/pallas_call | solution.py:566
  68.6 1.2 %copy.15 = f32[1,4]{1,0:T(1,128)} copy(f32[1,4]{1,0:T(1,128)} %get-tuple-element.6) | data formatting | bytes 32
  69.7 1.6 %copy.16 = f32[4,16,512]{2,1,0:T(8,128)} copy(f32[4,16,512]{2,1,0:T(8,128)} %get-tuple-element.7) | data formatting | bytes 262144
  71.3 1.3 %copy.17 = f32[4,6]{1,0:T(4,128)} copy(f32[4,6]{1,0:T(4,128)} %get-tuple-element.8) | data formatting | bytes 192

commit v3 on v2

--- a/solution.py
+++ b/solution.py
@@ -62,9 +62,7 @@
     actw_hbm,
     gain_hbm,
     head_hbm,
-    q_ref,
-    grad_ref,
-    actgrad_ref,
+    out_ref,
     rows_all,
     weights,
     out_weight,
@@ -78,6 +76,8 @@
     hid_slots,
     fact_a_src,
     fact_a,
+    fact_c_src,
+    fact_c,
     fact_b_src,
     fact_b,
     extra_src,
@@ -85,9 +85,12 @@
     partial,
     sib_part,
     row_sum,
+    row_send,
     row_parts,
     act_pick,
     act_sum,
+    act_raw,
+    act_pad,
     len_ref,
     boot_ref,
     gain_ref,
@@ -128,6 +131,8 @@
 
     sibling = dev(y, z, CORES - 1 - core)
 
+    far_first = sorted(range(1, nz), key=lambda d: -min(d, nz - d))
+
     loads = [
         pltpu.make_async_copy(src, dst, local_sem.at[i])
         for i, (src, dst) in enumerate(
@@ -138,7 +143,7 @@
                 (project_hbm.at[2], weights.at[2]),
                 (project_hbm.at[0], weights.at[0]),
                 (out_hbm, out_weight),
-                (act_hbm, act_slots.at[zh, yk]),
+                (act_hbm, act_raw),
                 (len_hbm, len_ref),
                 (boot_hbm, boot_ref),
                 (gain_hbm, gain_ref),
@@ -284,42 +289,61 @@
     for d in range(1, ny):
         ref = block_at(far, z, y)
         far_y.append(push(ref, ref, dev_y(mod(y + d, ny))))
+    loads[6].wait()
+    act_pad[...] = jnp.zeros_like(act_pad)
+    act_pad[0:seqs, 0:act_len] = act_raw[...].astype(f32)
+    act_slots[zh, yk] = act_pad[...].astype(bf16)
+    act_sem = push(act_slots.at[zh, yk], act_slots.at[zh, yk], dev_z(mod(z + nt, nz)))
     waiting = [spread_y(z)]
-    loads[6].wait()
-    act_sem = push(act_slots.at[zh, yk], act_slots.at[zh, yk], dev_z(mod(z + nt, nz)))
+    rest = far_rings[1:]
+    owners_at = {}
+
+    def lead_step(step):
+        got = near_recv(step)
+        if step + 1 < ring_steps:
+            near_send(step + 1)
+        owners_at[step] = far_rings[0][1](step)
+        if step + 1 < ring_steps:
+            far_rings[0][0](step + 1)
+        waiting.extend(spread_y(owner) for owner in got)
+
+    def rest_step(step):
+        owners = owners_at[step]
+        for send, recv, _ in rest:
+            got = recv(step)
+            if step + 1 < ring_steps:
+                send(step + 1)
+            owners = got if len(got) > len(owners) else owners
+        if step + 1 < ring_steps or steps_up == steps_down:
+            shared_far.extend(share(far, owner) for owner in owners)
+        else:
+            shared_far.append(share(far, mod(z + ring_steps, nz)))
+
+    def finish_waiting(count):
+        for item in waiting[:count]:
+            finish_near(*item)
+        del waiting[:count]
+
+    lead_step(0)
     for d in range(1, ny):
         arrive(block_at(far, z, mod(y - d, ny)), far_y[d - 1])
         far_rings[d][0](0)
     shared_far.append(share(far, z))
     for step in range(ring_steps):
-        got = near_recv(step)
         if step + 1 < ring_steps:
-            near_send(step + 1)
-        came = [spread_y(owner) for owner in got]
-        far_got = []
-        for send, recv, _ in far_rings:
-            owners = recv(step)
-            if step + 1 < ring_steps:
-                send(step + 1)
-            far_got = owners if len(owners) > len(far_got) else far_got
-        if step + 1 < ring_steps:
-            shared_far.extend(share(far, owner) for owner in far_got)
-        for item in waiting:
-            finish_near(*item)
-        waiting = came
+            lead_step(step + 1)
+        rest_step(step)
         if step == 0:
             arrive(act_slots.at[1 - zh, yk], act_sem)
             for d in range(1, nyk):
                 ref = act_slots.at[:, yk]
                 act_sems.append(push(ref, ref, dev_yk(mod(yk + d, nyk))))
-        if step == 2:
+            finish_waiting(1)
+        else:
+            finish_waiting(2)
+        if step == 1:
             prepare_actions()
-    for item in waiting:
-        finish_near(*item)
-    if steps_up == steps_down:
-        shared_far.extend(share(far, owner) for owner in far_got)
-    else:
-        shared_far.append(share(far, mod(z + ring_steps, nz)))
+    finish_waiting(len(waiting))
 
     def position(index):
         zh_at = lax.div(index, half)
@@ -332,39 +356,18 @@
     lane_pos = position(iota((16, hist), 1))
     row_pos = position(iota((hist, 128), 0))
 
-    def project(b):
-        last = len_ref[b] - 1
-        pick = (lane_pos == last).astype(f32).astype(bf16)
-        is_last = row_pos == last
-        blocks = [rows_all[b, g].reshape(hist, feats) for g in range(nt)]
-        own = jnp.concatenate([dot(pick, block) for block in blocks], axis=1)
-        full = own[0:8] + embedded[b : b + 1, :]
-        last_f32[b : b + 1, :] = full[0:1]
-        full_bf = full.astype(bf16).astype(f32)
-        key_sum = jnp.zeros((hist, inner), f32)
-        value_sum = jnp.zeros((hist, inner), f32)
-        for g in range(nt):
-            cut = slice(g * feats, (g + 1) * feats)
-            mark = jnp.concatenate([is_last] * (feats // 128), axis=1)
-            block = jnp.where(mark, full_bf[0:1, cut], blocks[g].astype(f32)).astype(bf16)
-            key_sum += dot(block, weights[1, cut, :])
-            value_sum += dot(block, weights[2, cut, :])
-        keys[b] = key_sum.astype(bf16)
-        values[b] = value_sum.astype(bf16)
-
     last_f32[...] = jnp.zeros_like(last_f32)
-    for dst, sem in shared_near:
+    for dst, sem in shared_near + shared_far:
         arrive(dst, sem)
-    for b in range(first):
-        project(b)
-    for dst, sem in shared_far:
-        arrive(dst, sem)
-    for b in range(first, seqs):
-        project(b)
-
+    for b in range(seqs):
+        pick = (lane_pos == len_ref[b] - 1).astype(f32).astype(bf16)
+        own = [dot(pick, rows_all[b, g].reshape(hist, feats)) for g in range(nt)]
+        full = jnp.concatenate(own, axis=1)[0:1] + embedded[b : b + 1, :]
+        last_f32[b : b + 1, :] = full
+    last_rows = last_f32[...]
+    last_round = last_rows.astype(bf16).astype(f32)
+    last_bf[...] = jnp.concatenate([last_round, jnp.zeros_like(last_round)], axis=0).astype(bf16)
     loads[4].wait()
-    last_rows = last_f32[...]
-    last_bf[...] = jnp.concatenate([last_rows, jnp.zeros_like(last_rows)], axis=0).astype(bf16)
     query = dot(last_bf[...], weights[0])[0:8]
     row_id = iota((rows, inner), 0)
     row_head = lax.rem(row_id, heads) == lax.div(iota((rows, inner), 1), HEAD_DIM)
@@ -393,6 +396,32 @@
         return out
 
     query_rows = spread(query)
+    key_vec = dot_split(query_rows, weights[1], NT_DIMS) * scale
+    for g in range(nt):
+        fact_a_src[g] = key_vec[:, g * feats : (g + 1) * feats].astype(bf16)
+    fact_a[z] = fact_a_src[group]
+    a_sems = {}
+    for d in far_first:
+        to = mod(z + d, nz)
+        a_sems[d] = push(fact_a_src.at[lax.rem(to, nt)], fact_a.at[z], dev_z(to))
+
+    def project(b):
+        is_last = row_pos == len_ref[b] - 1
+        mark = jnp.concatenate([is_last] * (feats // 128), axis=1)
+        key_sum = jnp.zeros((hist, inner), f32)
+        value_sum = jnp.zeros((hist, inner), f32)
+        for g in range(nt):
+            cut = slice(g * feats, (g + 1) * feats)
+            block = rows_all[b, g].reshape(hist, feats).astype(f32)
+            block = jnp.where(mark, last_round[b : b + 1, cut], block).astype(bf16)
+            key_sum += dot(block, weights[1, cut, :])
+            value_sum += dot(block, weights[2, cut, :])
+        keys[b] = key_sum.astype(bf16)
+        values[b] = value_sum.astype(bf16)
+
+    for b in range(seqs):
+        project(b)
+
     scores = per_seq((rows, hist), lambda b: dot_split(query_rows, keys[b], NT_DIMS)) * scale
     seq_row = lax.div(iota((rows, hist), 0), heads)
     pos = position(iota((rows, hist), 1))
@@ -409,32 +438,30 @@
     loads[5].wait()
     attended_bf = jnp.concatenate([attended, jnp.zeros_like(attended)], axis=0).astype(bf16)
     head_part = dot(attended_bf, out_weight[...])
-    hid_slots[group, 0:seqs, :] = head_part[0:seqs, : width // 2]
-    hid_slots[group, seqs : 2 * seqs, :] = head_part[0:seqs, width // 2 :]
+    quarter = width // 4
+    hid_slots[group] = jnp.concatenate(
+        [head_part[0:seqs, j * quarter : (j + 1) * quarter] for j in range(4)], axis=0
+    ).astype(bf16)
     hid_sems = []
     for d in range(1, nt):
         to = mod(group + d, nt)
         hid_sems.append(push(hid_slots.at[group], hid_slots.at[group], dev_z(zh * nt + to)))
 
-    key_vec = dot_split(query_rows, weights[1], NT_DIMS) * scale
-    for z_at in range(nz):
-        g = z_at % nt
-        h = z_at // nt
-        fact_a_src[z_at, :, :feats] = key_vec[:, g * feats : (g + 1) * feats].astype(bf16)
-        fact_a_src[z_at, :, feats:] = attention_round[:, h * half : (h + 1) * half]
-    fact_a[z] = fact_a_src[z]
-    a_sems = []
-    for d in range(1, nz):
+    for h in range(HALVES):
+        fact_c_src[h] = attention_round[:, h * half : (h + 1) * half]
+    fact_c[z] = fact_c_src[zh]
+    c_sems = {}
+    for d in far_first:
         to = mod(z + d, nz)
-        a_sems.append(push(fact_a_src.at[to], fact_a.at[z], dev_z(to)))
+        c_sems[d] = push(fact_c_src.at[lax.div(to, nt)], fact_c.at[z], dev_z(to))
 
     for d in range(1, nt):
         arrive(hid_slots.at[mod(group - d, nt)], hid_sems[d - 1])
-    total = hid_slots[0]
+    total = hid_slots[0].astype(f32)
     for g in range(1, nt):
-        total = total + hid_slots[g]
+        total = total + hid_slots[g].astype(f32)
     zero_rows = jnp.zeros((8 - seqs, width), f32)
-    head_sum = jnp.concatenate([total[0:seqs], total[seqs : 2 * seqs]], axis=1)
+    head_sum = jnp.concatenate([total[j * seqs : (j + 1) * seqs] for j in range(4)], axis=1)
     hidden = last_rows + jnp.concatenate([head_sum, zero_rows], axis=0)
     gain_head = gain_ref[...] * head_ref[...]
     inverse = lax.rsqrt(jnp.sum(hidden * hidden, axis=1, keepdims=True) * (1.0 / width) + NORM_EPS)
@@ -443,7 +470,6 @@
     q_lane = iota((8, 128), 1)
     q_row = iota((8, 128), 0)
     q_line = jnp.sum(jnp.where(q_lane == q_row, q_vals, 0.0), axis=0, keepdims=True)
-    q_ref[...] = q_line[:, 0:seqs]
     boot = jnp.zeros((8, 1), f32)
     for b in range(seqs):
         boot = jnp.where(iota((8, 1), 0) == b, boot_ref[0, b].astype(f32), boot)
@@ -463,10 +489,10 @@
         fact_b_src[z_at, :, :feats] = value_vec[:, g * feats : (g + 1) * feats].astype(bf16)
         fact_b_src[z_at, :, feats:] = grad_scores[:, h * half : (h + 1) * half].astype(bf16)
     fact_b[z] = fact_b_src[z]
-    b_sems = []
-    for d in range(1, nz):
+    b_sems = {}
+    for d in far_first:
         to = mod(z + d, nz)
-        b_sems.append(push(fact_b_src.at[to], fact_b.at[z], dev_z(to)))
+        b_sems[d] = (push(fact_b_src.at[to], fact_b.at[z], dev_z(to)))
 
     grad_query = per_seq((rows, inner), lambda b: dot_split(grad_scores, keys[b]))
     grad_query = fold(jnp.where(row_head, grad_query, 0.0)) * scale
@@ -487,61 +513,87 @@
         extra_src[z_at, seqs : 2 * seqs, :cut] = extra_rows[0:seqs, g * feats + cut : (g + 1) * feats]
         extra_src[z_at, :, cut:] = act_cols[:, z_at * 128 : (z_at + 1) * 128]
     extra[z] = extra_src[z]
-    x_sems = []
+    x_sems = {}
+    for d in far_first:
+        to = mod(z + d, nz)
+        x_sems[d] = (push(extra_src.at[to], extra.at[z], dev_z(to)))
+
     for d in range(1, nz):
-        to = mod(z + d, nz)
-        x_sems.append(push(extra_src.at[to], extra.at[z], dev_z(to)))
-
+        arrive(fact_a.at[mod(z - d, nz)], a_sems[d])
+        arrive(fact_c.at[mod(z - d, nz)], c_sems[d])
     for d in range(1, nz):
-        arrive(fact_a.at[mod(z - d, nz)], a_sems[d - 1])
-    for d in range(1, nz):
-        arrive(fact_b.at[mod(z - d, nz)], b_sems[d - 1])
+        arrive(fact_b.at[mod(z - d, nz)], b_sems[d])
     factors = nz * rows
-    vec_a = fact_a[:, :, :feats].reshape(factors, feats)
+    vec_a = fact_a[...].reshape(factors, feats)
     vec_b = fact_b[:, :, :feats].reshape(factors, feats)
     coef_a = fact_b[:, :, feats:].reshape(factors, half).astype(f32)
-    coef_b = fact_a[:, :, feats:].reshape(factors, half).astype(f32)
+    coef_b = fact_c[...].reshape(factors, half).astype(f32)
     coefs = jnp.concatenate([coef_a.T, coef_b.T], axis=1)
     vecs = jnp.concatenate([vec_a, vec_b], axis=0)
     seq_col = lax.div(lax.rem(iota(coefs.shape, 1), rows), heads)
+    y_sems = {}
+    sib_sems = {}
+
+    def multiply(b):
+        out = dot(jnp.where(seq_col == b, coefs, 0.0).astype(bf16), vecs)
+        partial[b] = out.reshape(ny, CORES, steps, feats)
+        sib_sems[b] = push(partial.at[b, :, other], sib_part.at[b], sibling)
+
+    def over_y(b):
+        arrive(sib_part.at[b], sib_sems[b])
+        total = partial[b, :, core] + sib_part[b]
+        row_sum[b] = total
+        row_send[b] = total.astype(bf16)
+        for d in range(1, ny):
+            y_sems[b, d] = push(
+                row_send.at[b, mod(y + d, ny)], row_parts.at[d - 1, b], dev_y(mod(y + d, ny))
+            )
+
+    multiply(0)
+    multiply(1)
+    over_y(0)
+    multiply(2)
+    over_y(1)
     for d in range(1, nz):
-        arrive(extra.at[mod(z - d, nz)], x_sems[d - 1])
+        arrive(extra.at[mod(z - d, nz)], x_sems[d])
     extra_sum = extra[0]
     for z_at in range(1, nz):
         extra_sum = extra_sum + extra[z_at]
-    act_sum[yk] = extra_sum[:, cut:]
+    act_sum[yk] = extra_sum
     act_sems = []
     for d in range(1, nyk):
         act_sems.append(push(act_sum.at[yk], act_sum.at[yk], dev_yk(mod(yk + d, nyk))))
-    extra_full = jnp.concatenate([extra_sum[0:seqs, :cut], extra_sum[seqs : 2 * seqs, :cut]], axis=1)
-    here = position(iota((half, feats), 0) + zh * half)
-    for b in range(seqs):
-        out = dot(jnp.where(seq_col == b, coefs, 0.0).astype(bf16), vecs)
-        out = out + jnp.where(here == len_ref[b] - 1, extra_full[b : b + 1, :], 0.0)
-        partial[:, :, b] = out.reshape(ny, CORES, steps, feats)
-
-    sib_sem = push(partial.at[:, other], sib_part, sibling)
-    arrive(sib_part, sib_sem)
-    row_sum[...] = partial[:, core] + sib_part[...]
-    y_sems = []
-    for d in range(1, ny):
-        to = mod(y + d, ny)
-        y_sems.append(push(row_sum.at[to], row_parts.at[d - 1], dev_y(to)))
+    multiply(3)
+    over_y(2)
+    over_y(3)
+
     for d in range(1, nyk):
         arrive(act_sum.at[mod(yk - d, nyk)], act_sems[d - 1])
     act_total = act_sum[0]
     for yk_at in range(1, nyk):
         act_total = act_total + act_sum[yk_at]
     mine = (iota((128, 128), 0) == iota((128, 128), 1) + yk * part) & (iota((128, 128), 1) < part)
-    act_mine = dot_exact(act_total, mine.astype(f32).astype(bf16))
-    actgrad_ref[...] = act_mine[0:seqs, 0:part]
-    result = row_sum[y]
-    for d in range(1, ny):
-        arrive(row_parts.at[d - 1], y_sems[d - 1])
-        result = result + row_parts[d - 1]
-    grad_ref[...] = result
+    act_mine = dot_exact(act_total[:, cut:], mine.astype(f32).astype(bf16))
+    out_ref[seqs * steps :, 0:128] = jnp.where(iota((8, 128), 0) == 0, q_line, 0.0)
+    out_ref[seqs * steps :, 128:256] = act_mine
+    here = iota((steps, feats), 0) + critic * steps
+    for b in range(seqs):
+        low = jnp.concatenate([act_total[b : b + 1, :cut], act_total[seqs + b : seqs + b + 1, :cut]], axis=1)
+        result = row_sum[b, y] + jnp.where(here == len_ref[b] - 1, low, 0.0)
+        for d in range(1, ny):
+            arrive(row_parts.at[d - 1, b], y_sems[b, d])
+            result = result + row_parts[d - 1, b].astype(f32)
+        out_ref[b * steps : (b + 1) * steps, :] = result
     for copy in sends:
         copy.wait_send()
+
+
+def unpack(packed, q_ref, grad_ref, actgrad_ref):
+    seqs, steps, feats = grad_ref.shape
+    tail = seqs * steps
+    q_ref[...] = packed[tail : tail + 1, 0:seqs]
+    grad_ref[...] = packed[0:tail, :].reshape(seqs, steps, feats)
+    actgrad_ref[...] = packed[tail : tail + seqs, 128 : 128 + actgrad_ref.shape[1]]
 
 
 def solution(mesh):
@@ -558,20 +610,15 @@
         hist = steps * HALVES * nyk
         half = steps * nyk
         weights = jnp.transpose(project[0], (1, 0, 2))
-        padded = jnp.pad(actions, ((0, 16 - seqs), (0, 128 - act_len)))
         vmem = pl.BlockSpec(memory_space=pltpu.VMEM)
         hbm = pl.BlockSpec(memory_space=pltpu.HBM)
         part = act_len // nt
         flops = 4 * seqs * hist * width * inner
-        return pl.pallas_call(
+        packed = pl.pallas_call(
             functools.partial(kernel, (ny, nt, seqs, steps, feats, inner, act_len)),
-            out_shape=(
-                jax.ShapeDtypeStruct((1, seqs), f32),
-                jax.ShapeDtypeStruct((seqs, steps, feats), f32),
-                jax.ShapeDtypeStruct((seqs, part), f32),
-            ),
+            out_shape=jax.ShapeDtypeStruct((seqs * steps + 8, feats), f32),
             in_specs=[hbm] * 9,
-            out_specs=(vmem, vmem, vmem),
+            out_specs=vmem,
             scratch_shapes=[
                 pltpu.VMEM((seqs, nt, HALVES, ny, CORES, steps, feats), bf16),
                 pltpu.VMEM((3, width, inner), bf16),
@@ -583,19 +630,24 @@
                 pltpu.VMEM((16, width), f32),
                 pltpu.VMEM((8, width), f32),
                 pltpu.VMEM((16, width), bf16),
-                pltpu.VMEM((nt, 8, width // 2), f32),
-                pltpu.VMEM((nz, rows, feats + half), bf16),
-                pltpu.VMEM((nz, rows, feats + half), bf16),
+                pltpu.VMEM((nt, 16, width // 4), bf16),
+                pltpu.VMEM((nt, rows, feats), bf16),
+                pltpu.VMEM((nz, rows, feats), bf16),
+                pltpu.VMEM((HALVES, rows, half), bf16),
+                pltpu.VMEM((nz, rows, half), bf16),
                 pltpu.VMEM((nz, rows, feats + half), bf16),
                 pltpu.VMEM((nz, rows, feats + half), bf16),
                 pltpu.VMEM((nz, 8, feats // 2 + 128), f32),
                 pltpu.VMEM((nz, 8, feats // 2 + 128), f32),
-                pltpu.VMEM((ny, CORES, seqs, steps, feats), f32),
-                pltpu.VMEM((ny, seqs, steps, feats), f32),
-                pltpu.VMEM((ny, seqs, steps, feats), f32),
-                pltpu.VMEM((ny - 1, seqs, steps, feats), f32),
+                pltpu.VMEM((seqs, ny, CORES, steps, feats), f32),
+                pltpu.VMEM((seqs, ny, steps, feats), f32),
+                pltpu.VMEM((seqs, ny, steps, feats), f32),
+                pltpu.VMEM((seqs, ny, steps, feats), bf16),
+                pltpu.VMEM((ny - 1, seqs, steps, feats), bf16),
                 pltpu.VMEM((act_weight.shape[1], nz * 128), bf16),
-                pltpu.VMEM((nyk, 8, 128), f32),
+                pltpu.VMEM((nyk, 8, feats // 2 + 128), f32),
+                pltpu.VMEM((seqs, act_len), bf16),
+                pltpu.VMEM((16, 128), f32),
                 pltpu.SMEM((seqs,), jnp.int32),
                 pltpu.SMEM((1, seqs), jnp.int32),
                 pltpu.VMEM((1, width), f32),
@@ -610,7 +662,17 @@
             cost_estimate=pl.CostEstimate(
                 flops=flops, bytes_accessed=10 * 1024 * 1024, transcendentals=seqs * hist
             ),
-        )(obs, padded, lengths, boot, weights, out_weight[0], act_weight[0], gain, head)
+        )(obs, actions, lengths, boot, weights, out_weight[0], act_weight[0], gain, head)
+        return pl.pallas_call(
+            unpack,
+            out_shape=(
+                jax.ShapeDtypeStruct((1, seqs), f32),
+                jax.ShapeDtypeStruct((seqs, steps, feats), f32),
+                jax.ShapeDtypeStruct((seqs, part), f32),
+            ),
+            in_specs=[vmem],
+            out_specs=(vmem, vmem, vmem),
+        )(packed)
 
     in_specs = (
         P("seq", "critic", "tensor"),

time: 72.9 us -> 64.4 us (0.88)
  local copies, waits for them, and re-layouts: 5.27 us -> 0 us
  Pallas kernels: 66.6 us -> 63.7 us
    pallas_call x1, Pallas kernels: 66.6 us -> 62.1 us  [on_device(): pl.pallas_call(functools.partial(kernel, (ny, nt, seqs, steps, feats, inn...]
    unnamed x3 -> x0, local copies, waits for them, and re-layouts: 3.99 us -> none
    pallas_call x0 -> x1, Pallas kernels: none -> 1.58 us  [on_device(): pl.pallas_call(unpack, out_shape=(jax.ShapeDtypeStruct((1, seqs), f32), j...]
    pad x1 -> x0, local copies, waits for them, and re-layouts: 1.28 us -> none  [on_device(): padded = jnp.pad(actions, ((0, 16 - seqs), (0, 128 - act_len)))]
where the time goes in v3:
time: 64.4 us; the launch traced here: 64.3 us
  Pallas kernels  63.7 us (99%)
    pallas_call x1, Pallas kernels, on_device(): pl.pallas_call(functools.partial(kernel, (ny, nt, seqs, steps, feats, inn...  62.1 us
    pallas_call x1, Pallas kernels, on_device(): pl.pallas_call(unpack, out_shape=(jax.ShapeDtypeStruct((1, seqs), f32), j...  1.58 us

profile of v3, /device:TPU:1, one launch (start us, length us, event | category | flops | bytes accessed | tf_op | source)
XLA Modules:
  0.0 64.3 jit_solution(7344365161193947312)
XLA Ops:
  0.6 62.1 %shard_map.112.packed = f32[72,512]{1,0:T(8,128)} custom-call(bf16[4,16,512]{2,1,0:T(8,128)(2,1)} %obs_hbm.1, bf16[4,24]{1,0:T(4,128)(2,1)} %act_hbm.1, s32[4]{0:T(128)} %len_hbm.1, s32[1,4]{1,0:T(1,128)} %boot_hbm.1, bf16[3,2048,512]{2,1,0:T(8,128)(2,1)} %bitcast.5, bf16[512,2048]{1,0:T(8,128)(2,1)} %bitcast.6, bf16[384,2048]{1,0:T(8,128)(2,1)} %bitcast.7, ...), custom_call_target="tpu_custom_call" | custom-call | flops 4294967296 | bytes 10485760 | tf_op jit(solution)/shard_map/pallas_call | solution.py:617
  62.7 1.6 %shard_map.113 = (f32[1,4]{1,0:T(1,128)}, f32[4,16,512]{2,1,0:T(8,128)}, f32[4,6]{1,0:T(4,128)}) custom-call(f32[72,512]{1,0:T(8,128)} %shard_map.112.packed), custom_call_target="tpu_custom_call" | custom-call | tf_op jit(solution)/shard_map/pallas_call | solution.py:666

commit v4 on v3

--- a/solution.py
+++ b/solution.py
@@ -67,6 +67,7 @@
     weights,
     out_weight,
     act_weight,
+    act_ring,
     act_slots,
     keys,
     values,
@@ -155,14 +156,10 @@
         load.start()
 
     barrier = pltpu.get_barrier_semaphore()
-    for d in range(1, nz):
-        pl.semaphore_signal(
-            barrier, inc=1, device_id=dev_z(mod(z + d, nz)), device_id_type=pl.DeviceIdType.MESH
-        )
-    for d in range(1, nyk):
-        pl.semaphore_signal(
-            barrier, inc=1, device_id=dev_yk(mod(yk + d, nyk)), device_id_type=pl.DeviceIdType.MESH
-        )
+    greeted = [dev_z(mod(z + d, nz)) for d in sorted({1, nz - 1})]
+    greeted += [dev(mod(y + d, ny), z, core) for d in range(1, ny)] + [sibling]
+    for target in greeted:
+        pl.semaphore_signal(barrier, inc=1, device_id=target, device_id_type=pl.DeviceIdType.MESH)
 
     part = act_len // nt
     pick_shape = act_pick.shape
@@ -177,6 +174,11 @@
 
     sends = []
     sem_at = [0]
+
+    def drain(count):
+        for copy in sends[:count]:
+            copy.wait_send()
+        del sends[:count]
 
     def copy_of(src, dst, target, sem):
         return pltpu.make_async_remote_copy(
@@ -246,11 +248,12 @@
     steps_up = nz // 2
     steps_down = (nz - 1) // 2
     near_ring = ring(z, nz, lambda z_at: block_at(near, z_at, y), dev_z, steps_up, steps_down)
-    far_rings = []
+    near_first = sorted(range(1, ny), key=lambda d: min(d, ny - d))
+    far_rings = {}
     for d in range(ny):
         y_at = mod(y - d, ny)
         ups, downs = (steps_up, steps_down) if d % 2 else (steps_down, steps_up)
-        far_rings.append(
+        far_rings[d] = (
             ring(z, nz, functools.partial(lambda y_at, z_at: block_at(far, z_at, y_at), y_at), dev_z, ups, downs)
         )
     ring_steps = max(steps_up, steps_down)
@@ -265,9 +268,7 @@
         shared_near.append(share(near, owner))
 
     def prepare_actions():
-        for d in range(1, nyk):
-            arrive(act_slots.at[:, mod(yk - d, nyk)], act_sems[d - 1])
-        act_part = act_slots.shape[3]
+        act_part = act_slots.shape[4]
         gathered = jnp.zeros((16, act_weight.shape[0]), f32)
         lane = iota((act_part, act_weight.shape[0]), 1)
         lane_row = iota((act_part, act_weight.shape[0]), 0)
@@ -275,12 +276,12 @@
             for yk_at in range(nyk):
                 c = (yk_at // CORES * HALVES + zh_at) * CORES + yk_at % CORES
                 place = (lane == lane_row + c * act_len) & (lane_row < act_len)
-                gathered += dot(act_slots[zh_at, yk_at], place.astype(f32).astype(bf16))
+                gathered += dot(act_slots[zh_at, yk_at // CORES, yk_at % CORES], place.astype(f32).astype(bf16))
 
         loads[1].wait()
         embedded[...] = dot(gathered.astype(bf16), act_weight[...])
 
-    pl.semaphore_wait(barrier, nz - 1 + nyk - 1)
+    pl.semaphore_wait(barrier, len(greeted))
     loads[0].wait()
     near_send, near_recv, _ = near_ring
     near_send(0)
@@ -292,10 +293,19 @@
     loads[6].wait()
     act_pad[...] = jnp.zeros_like(act_pad)
     act_pad[0:seqs, 0:act_len] = act_raw[...].astype(f32)
-    act_slots[zh, yk] = act_pad[...].astype(bf16)
-    act_sem = push(act_slots.at[zh, yk], act_slots.at[zh, yk], dev_z(mod(z + nt, nz)))
+    act_ring[z] = act_pad[...].astype(bf16)
+    act_sem = {}
+
+    def act_step(step):
+        if step > 0:
+            arrive(act_ring.at[mod(z - step, nz)], act_sem[step - 1])
+        if step < nt:
+            ref = act_ring.at[mod(z - step, nz)]
+            act_sem[step] = push(ref, ref, dev_z(mod(z + 1, nz)))
+
+    act_step(0)
     waiting = [spread_y(z)]
-    rest = far_rings[1:]
+    rest = [far_rings[d] for d in near_first]
     owners_at = {}
 
     def lead_step(step):
@@ -305,6 +315,7 @@
         owners_at[step] = far_rings[0][1](step)
         if step + 1 < ring_steps:
             far_rings[0][0](step + 1)
+        act_step(step + 1)
         waiting.extend(spread_y(owner) for owner in got)
 
     def rest_step(step):
@@ -325,7 +336,7 @@
         del waiting[:count]
 
     lead_step(0)
-    for d in range(1, ny):
+    for d in near_first:
         arrive(block_at(far, z, mod(y - d, ny)), far_y[d - 1])
         far_rings[d][0](0)
     shared_far.append(share(far, z))
@@ -333,17 +344,19 @@
         if step + 1 < ring_steps:
             lead_step(step + 1)
         rest_step(step)
-        if step == 0:
-            arrive(act_slots.at[1 - zh, yk], act_sem)
-            for d in range(1, nyk):
-                ref = act_slots.at[:, yk]
-                act_sems.append(push(ref, ref, dev_yk(mod(yk + d, nyk))))
-            finish_waiting(1)
-        else:
-            finish_waiting(2)
-        if step == 1:
-            prepare_actions()
+        if step + 2 == ring_steps:
+            act_slots[zh, y, core] = act_ring[z]
+            act_slots[1 - zh, y, core] = act_ring[mod(z - nt, nz)]
+            for d in range(1, ny):
+                ref = act_slots.at[:, y, core]
+                act_sems.append(push(ref, ref, dev_y(mod(y + d, ny))))
+        finish_waiting(1 if step == 0 else 2)
+    for d in range(1, ny):
+        arrive(act_slots.at[:, mod(y - d, ny), core], act_sems[d - 1])
+    act_share = push(act_slots.at[:, :, core], act_slots.at[:, :, core], sibling)
     finish_waiting(len(waiting))
+    arrive(act_slots.at[:, :, other], act_share)
+    prepare_actions()
 
     def position(index):
         zh_at = lax.div(index, half)
@@ -455,6 +468,8 @@
         to = mod(z + d, nz)
         c_sems[d] = push(fact_c_src.at[lax.div(to, nt)], fact_c.at[z], dev_z(to))
 
+    for d in range(1, nz):
+        arrive(fact_a.at[mod(z - d, nz)], a_sems[d])
     for d in range(1, nt):
         arrive(hid_slots.at[mod(group - d, nt)], hid_sems[d - 1])
     total = hid_slots[0].astype(f32)
@@ -489,6 +504,7 @@
         fact_b_src[z_at, :, :feats] = value_vec[:, g * feats : (g + 1) * feats].astype(bf16)
         fact_b_src[z_at, :, feats:] = grad_scores[:, h * half : (h + 1) * half].astype(bf16)
     fact_b[z] = fact_b_src[z]
+    before_b = len(sends)
     b_sems = {}
     for d in far_first:
         to = mod(z + d, nz)
@@ -518,18 +534,18 @@
         to = mod(z + d, nz)
         x_sems[d] = (push(extra_src.at[to], extra.at[z], dev_z(to)))
 
+    drain(before_b)
+    factors = nz * rows
     for d in range(1, nz):
-        arrive(fact_a.at[mod(z - d, nz)], a_sems[d])
         arrive(fact_c.at[mod(z - d, nz)], c_sems[d])
+    coef_b = fact_c[...].reshape(factors, half).astype(f32).T
     for d in range(1, nz):
         arrive(fact_b.at[mod(z - d, nz)], b_sems[d])
-    factors = nz * rows
-    vec_a = fact_a[...].reshape(factors, feats)
-    vec_b = fact_b[:, :, :feats].reshape(factors, feats)
-    coef_a = fact_b[:, :, feats:].reshape(factors, half).astype(f32)
-    coef_b = fact_c[...].reshape(factors, half).astype(f32)
-    coefs = jnp.concatenate([coef_a.T, coef_b.T], axis=1)
-    vecs = jnp.concatenate([vec_a, vec_b], axis=0)
+    coef_a = fact_b[:, :, feats:].reshape(factors, half).astype(f32).T
+    coefs = jnp.concatenate([coef_a, coef_b], axis=1)
+    vecs = jnp.concatenate(
+        [fact_a[...].reshape(factors, feats), fact_b[:, :, :feats].reshape(factors, feats)], axis=0
+    )
     seq_col = lax.div(lax.rem(iota(coefs.shape, 1), rows), heads)
     y_sems = {}
     sib_sems = {}
@@ -566,6 +582,7 @@
     multiply(3)
     over_y(2)
     over_y(3)
+    drain(2 * (nz - 1))
 
     for d in range(1, nyk):
         arrive(act_sum.at[mod(yk - d, nyk)], act_sems[d - 1])
@@ -584,8 +601,7 @@
             arrive(row_parts.at[d - 1, b], y_sems[b, d])
             result = result + row_parts[d - 1, b].astype(f32)
         out_ref[b * steps : (b + 1) * steps, :] = result
-    for copy in sends:
-        copy.wait_send()
+    drain(len(sends))
 
 
 def unpack(packed, q_ref, grad_ref, actgrad_ref):
@@ -624,7 +640,8 @@
                 pltpu.VMEM((3, width, inner), bf16),
                 pltpu.VMEM((inner, width), bf16),
                 pltpu.VMEM(act_weight.shape[1:], bf16),
-                pltpu.VMEM((HALVES, nyk, 16, 128), bf16),
+                pltpu.VMEM((nz, 16, 128), bf16),
+                pltpu.VMEM((HALVES, ny, CORES, 16, 128), bf16),
                 pltpu.VMEM((seqs, hist, inner), bf16),
                 pltpu.VMEM((seqs, hist, inner), bf16),
                 pltpu.VMEM((16, width), f32),

time: 64.4 us -> 63.2 us (0.981)
  Pallas kernels: 63.7 us -> 62.5 us
    pallas_call x1, Pallas kernels: 62.1 us -> 60.9 us  [on_device(): pl.pallas_call(functools.partial(kernel, (ny, nt, seqs, steps, feats, inn...]
where the time goes in v4:
time: 63.2 us; the launch traced here: 63.1 us
  Pallas kernels  62.5 us (99%)
  between operations  0.64 us (1%)
    pallas_call x1, Pallas kernels, on_device(): pl.pallas_call(functools.partial(kernel, (ny, nt, seqs, steps, feats, inn...  60.9 us
    pallas_call x1, Pallas kernels, on_device(): pl.pallas_call(unpack, out_shape=(jax.ShapeDtypeStruct((1, seqs), f32), j...  1.58 us

profile of v4, /device:TPU:1, one launch (start us, length us, event | category | flops | bytes accessed | tf_op | source)
XLA Modules:
  0.0 63.1 jit_solution(18103154278968105175)
XLA Ops:
  0.6 60.9 %shard_map.112.packed = f32[72,512]{1,0:T(8,128)} custom-call(bf16[4,16,512]{2,1,0:T(8,128)(2,1)} %obs_hbm.1, bf16[4,24]{1,0:T(4,128)(2,1)} %act_hbm.1, s32[4]{0:T(128)} %len_hbm.1, s32[1,4]{1,0:T(1,128)} %boot_hbm.1, bf16[3,2048,512]{2,1,0:T(8,128)(2,1)} %bitcast.5, bf16[512,2048]{1,0:T(8,128)(2,1)} %bitcast.6, bf16[384,2048]{1,0:T(8,128)(2,1)} %bitcast.7, ...), custom_call_target="tpu_custom_call" | custom-call | flops 4294967296 | bytes 10485760 | tf_op jit(solution)/shard_map/pallas_call | solution.py:633
  61.5 1.6 %shard_map.113 = (f32[1,4]{1,0:T(1,128)}, f32[4,16,512]{2,1,0:T(8,128)}, f32[4,6]{1,0:T(4,128)}) custom-call(f32[72,512]{1,0:T(8,128)} %shard_map.112.packed), custom_call_target="tpu_custom_call" | custom-call | tf_op jit(solution)/shard_map/pallas_call | solution.py:683

commit v5 on v4

--- a/solution.py
+++ b/solution.py
@@ -81,6 +81,8 @@
     fact_c,
     fact_b_src,
     fact_b,
+    fact_d_src,
+    fact_d,
     extra_src,
     extra,
     partial,
@@ -494,21 +496,25 @@
 
     grad_heads = spread(dot_split(grad_last, out_weight[...], NT_DIMS))
     value_vec = dot_split(grad_heads, weights[2], NT_DIMS)
+    before_b = len(sends)
+    for g in range(nt):
+        fact_b_src[g] = value_vec[:, g * feats : (g + 1) * feats].astype(bf16)
+    fact_b[z] = fact_b_src[group]
+    b_sems = {}
+    for d in far_first:
+        to = mod(z + d, nz)
+        b_sems[d] = push(fact_b_src.at[lax.rem(to, nt)], fact_b.at[z], dev_z(to))
     grad_attention = per_seq((rows, hist), lambda b: dot_split(grad_heads, values[b], NT_DIMS))
     grad_scores = attention * (
         grad_attention - jnp.sum(attention * grad_attention, axis=1, keepdims=True)
     )
-    for z_at in range(nz):
-        g = z_at % nt
-        h = z_at // nt
-        fact_b_src[z_at, :, :feats] = value_vec[:, g * feats : (g + 1) * feats].astype(bf16)
-        fact_b_src[z_at, :, feats:] = grad_scores[:, h * half : (h + 1) * half].astype(bf16)
-    fact_b[z] = fact_b_src[z]
-    before_b = len(sends)
-    b_sems = {}
+    for h in range(HALVES):
+        fact_d_src[h] = grad_scores[:, h * half : (h + 1) * half].astype(bf16)
+    fact_d[z] = fact_d_src[zh]
+    d_sems = {}
     for d in far_first:
         to = mod(z + d, nz)
-        b_sems[d] = (push(fact_b_src.at[to], fact_b.at[z], dev_z(to)))
+        d_sems[d] = push(fact_d_src.at[lax.div(to, nt)], fact_d.at[z], dev_z(to))
 
     grad_query = per_seq((rows, inner), lambda b: dot_split(grad_scores, keys[b]))
     grad_query = fold(jnp.where(row_head, grad_query, 0.0)) * scale
@@ -541,10 +547,11 @@
     coef_b = fact_c[...].reshape(factors, half).astype(f32).T
     for d in range(1, nz):
         arrive(fact_b.at[mod(z - d, nz)], b_sems[d])
-    coef_a = fact_b[:, :, feats:].reshape(factors, half).astype(f32).T
+        arrive(fact_d.at[mod(z - d, nz)], d_sems[d])
+    coef_a = fact_d[...].reshape(factors, half).astype(f32).T
     coefs = jnp.concatenate([coef_a, coef_b], axis=1)
     vecs = jnp.concatenate(
-        [fact_a[...].reshape(factors, feats), fact_b[:, :, :feats].reshape(factors, feats)], axis=0
+        [fact_a[...].reshape(factors, feats), fact_b[...].reshape(factors, feats)], axis=0
     )
     seq_col = lax.div(lax.rem(iota(coefs.shape, 1), rows), heads)
     y_sems = {}
@@ -582,7 +589,7 @@
     multiply(3)
     over_y(2)
     over_y(3)
-    drain(2 * (nz - 1))
+    drain(3 * (nz - 1))
 
     for d in range(1, nyk):
         arrive(act_sum.at[mod(yk - d, nyk)], act_sems[d - 1])
@@ -652,8 +659,10 @@
                 pltpu.VMEM((nz, rows, feats), bf16),
                 pltpu.VMEM((HALVES, rows, half), bf16),
                 pltpu.VMEM((nz, rows, half), bf16),
-                pltpu.VMEM((nz, rows, feats + half), bf16),
-                pltpu.VMEM((nz, rows, feats + half), bf16),
+                pltpu.VMEM((nt, rows, feats), bf16),
+                pltpu.VMEM((nz, rows, feats), bf16),
+                pltpu.VMEM((HALVES, rows, half), bf16),
+                pltpu.VMEM((nz, rows, half), bf16),
                 pltpu.VMEM((nz, 8, feats // 2 + 128), f32),
                 pltpu.VMEM((nz, 8, feats // 2 + 128), f32),
                 pltpu.VMEM((seqs, ny, CORES, steps, feats), f32),

time: 63.2 us -> 63.8 us (level)
  no operation moved by 1% of the time
where the time goes in v5:
time: 63.8 us; the launch traced here: 63.7 us
  Pallas kernels  63 us (99%)
  between operations  0.64 us (1%)
    pallas_call x1, Pallas kernels, on_device(): pl.pallas_call(functools.partial(kernel, (ny, nt, seqs, steps, feats, inn...  61.4 us
    pallas_call x1, Pallas kernels, on_device(): pl.pallas_call(unpack, out_shape=(jax.ShapeDtypeStruct((1, seqs), f32), j...  1.58 us

profile of v5, /device:TPU:1, one launch (start us, length us, event | category | flops | bytes accessed | tf_op | source)
XLA Modules:
  0.0 63.7 jit_solution(5706659784135390074)
XLA Ops:
  0.6 61.4 %shard_map.112.packed = f32[72,512]{1,0:T(8,128)} custom-call(bf16[4,16,512]{2,1,0:T(8,128)(2,1)} %obs_hbm.1, bf16[4,24]{1,0:T(4,128)(2,1)} %act_hbm.1, s32[4]{0:T(128)} %len_hbm.1, s32[1,4]{1,0:T(1,128)} %boot_hbm.1, bf16[3,2048,512]{2,1,0:T(8,128)(2,1)} %bitcast.5, bf16[512,2048]{1,0:T(8,128)(2,1)} %bitcast.6, bf16[384,2048]{1,0:T(8,128)(2,1)} %bitcast.7, ...), custom_call_target="tpu_custom_call" | custom-call | flops 4294967296 | bytes 10485760 | tf_op jit(solution)/shard_map/pallas_call | solution.py:640
  62.1 1.6 %shard_map.113 = (f32[1,4]{1,0:T(1,128)}, f32[4,16,512]{2,1,0:T(8,128)}, f32[4,6]{1,0:T(4,128)}) custom-call(f32[72,512]{1,0:T(8,128)} %shard_map.112.packed), custom_call_target="tpu_custom_call" | custom-call | tf_op jit(solution)/shard_map/pallas_call | solution.py:692
